TPU v7x, 32 devices: a whole 2x2x4 slice. The times are simulated.
32 devices in a mesh: wide: 16 (over z, y, x), narrow: 2 (over core).
Axes of the slice: x: 2, y: 2, z: 4, core: 2. Of those that a mesh axis runs over, the one named last changes fastest.
Arguments:
- loads: bfloat16 [16, 2, 64, 1024], P('wide', 'narrow'), may hold values from -30 to 30
- flexibility: bfloat16 [16, 2, 1024, 1024], P('wide', 'narrow'), may hold values from -1 to 6
- dirichlet: bfloat16 [16, 2, 1024, 1024], P('wide', 'narrow'), may hold values from -1 to 6
- modes: bfloat16 [16, 2, 32, 1024], P('wide', 'narrow'), may hold values from -0.75 to 0.75
- coarse_inverse: bfloat16 [512, 512], P('wide', 'narrow'), may hold values from -1 to 4
- mode_counts: int32 [2, 16], replicated, may hold values from 1 to 32, 256 in all within a row
Outputs:
- multipliers: bfloat16 [16, 2, 64, 1024], P('wide', 'narrow')
- residual: bfloat16 [16, 2, 64, 1024], P('wide', 'narrow')
Inputs may be any that keep to these rules, and one draw needn't show every extreme that they name: `mode_counts`: each row of this array is one grid column; the counts of each grid column sum to exactly 256 in all, and the largest count of each grid column is exactly 32.
All inputs are finite; a program needn't handle non-finite values.
Results may differ from a plain program's by a relative error of at most 0.0087.
The roundings to bfloat16 on the way count: a program that leaves them out, or rounds other values in their place, can miss the bound.
Values may be sent and summed in bfloat16 or wider, within the bound.
A program may use at most 64 MiB of HBM per device.

v0:
```python
import jax
import jax.numpy as jnp
from jax import lax
from jax.sharding import PartitionSpec as P

ITERS = 2


def extended(block, sides, width):
    for axis, dim in sides:
        count = lax.axis_size(axis)
        forward = [(i, i + 1) for i in range(count - 1)]
        backward = [(target, source) for source, target in forward]
        low = lax.ppermute(
            lax.slice_in_dim(block, block.shape[dim] - width, None, axis=dim), axis, forward
        )
        high = lax.ppermute(lax.slice_in_dim(block, 0, width, axis=dim), axis, backward)
        block = jnp.concatenate([low, block, high], axis=dim)
    return block


def jump_faces(values):
    load_count, width = values.shape
    face_len = width // 4
    face_parts = values.reshape(load_count, 4, face_len)
    north_face = face_parts[:, 0]
    south_face = face_parts[:, 1]
    west_face = face_parts[:, 2]
    east_face = face_parts[:, 3]
    vertical = extended(jnp.stack([north_face, south_face]), (("wide", 0),), 1)
    sideways = extended(jnp.stack([west_face, east_face]), (("narrow", 0),), 1)
    from_above = vertical[0]
    from_below = vertical[3]
    from_west = sideways[0]
    from_east = sideways[3]
    nearby = jnp.stack([from_above, from_below, from_west, from_east], axis=1)
    return (face_parts.astype(jnp.float32) - nearby.astype(jnp.float32)).reshape(load_count, width)


def load_sums(left, right):
    return lax.psum(jnp.sum(left * right, axis=1), ("wide", "narrow"))


def shards(loads, flexibility, dirichlet, modes, coarse_inverse, mode_counts):
    local_loads = loads[0, 0]
    flex_block = flexibility[0, 0]
    precond_block = dirichlet[0, 0]
    mode_block = modes[0, 0]
    mode_slots = mode_block.shape[0]
    column_width = coarse_inverse.shape[1]
    row_total = lax.axis_size("wide")
    coarse_order = coarse_inverse.shape[0] * row_total
    row_index = lax.axis_index("wide")
    column = lax.axis_index("narrow")
    counts = lax.dynamic_index_in_dim(mode_counts, column, 0, keepdims=False)
    end_points = jnp.cumsum(counts)
    starts = end_points - counts
    position = jnp.arange(column_width, dtype=jnp.int32)
    owner_row = jnp.sum((end_points[None, :] <= position[:, None]).astype(jnp.int32), axis=1)
    slot_index = owner_row * mode_slots + position - jnp.take(starts, owner_row)
    rank_list = jnp.arange(mode_slots, dtype=jnp.int32)
    own_index = jnp.minimum(
        column * column_width + jnp.take(starts, row_index) + rank_list, coarse_order - 1
    )
    is_valid = rank_list < jnp.take(counts, row_index)

    def coarse_term(rounded):
        weights = lax.dot_general(
            rounded, mode_block, (((1,), (1,)), ((), ())), preferred_element_type=jnp.float32
        ).astype(jnp.bfloat16)
        padded = lax.all_gather(weights, "wide", axis=1, tiled=True)
        column_values = jnp.take(padded, slot_index, axis=1)
        partial_values = lax.dot_general(
            column_values,
            coarse_inverse,
            (((1,), (1,)), ((), ())),
            preferred_element_type=jnp.float32,
        )
        block_values = lax.psum(partial_values, "narrow").astype(jnp.bfloat16)
        coarse_values = lax.all_gather(block_values, "wide", axis=1, tiled=True)
        picked = jnp.take(coarse_values, own_index, axis=1)
        picked = jnp.where(is_valid[None, :], picked, jnp.zeros_like(picked))
        return jnp.dot(picked, mode_block, preferred_element_type=jnp.float32)

    def precondition(values):
        rounded = values.astype(jnp.bfloat16)
        inner = jump_faces(rounded).astype(jnp.bfloat16)
        smoothed = jnp.dot(inner, precond_block, preferred_element_type=jnp.float32).astype(
            jnp.bfloat16
        )
        return jump_faces(smoothed) + coarse_term(rounded)

    disp = jnp.dot(local_loads, flex_block, preferred_element_type=jnp.float32).astype(jnp.bfloat16)
    residual = jump_faces(disp)
    multipliers = jnp.zeros_like(residual)
    direction = precondition(residual)
    energy = load_sums(residual, direction)
    for step_number in range(ITERS):
        moved = jump_faces(direction.astype(jnp.bfloat16)).astype(jnp.bfloat16)
        image = jump_faces(
            jnp.dot(moved, flex_block, preferred_element_type=jnp.float32).astype(jnp.bfloat16)
        )
        step_size = energy / load_sums(direction, image)
        multipliers = multipliers + step_size[:, None] * direction
        residual = residual - step_size[:, None] * image
        if step_number + 1 < ITERS:
            fresh_z = precondition(residual)
            fresh = load_sums(residual, fresh_z)
            direction = fresh_z + (fresh / energy)[:, None] * direction
            energy = fresh
    return (multipliers.astype(jnp.bfloat16)[None, None], residual.astype(jnp.bfloat16)[None, None])


def solution(mesh):
    return jax.shard_map(
        shards,
        mesh=mesh,
        in_specs=(
            P("wide", "narrow", None, None),
            P("wide", "narrow", None, None),
            P("wide", "narrow", None, None),
            P("wide", "narrow", None, None),
            P("wide", "narrow"),
            P(),
        ),
        out_specs=(P("wide", "narrow", None, None), P("wide", "narrow", None, None)),
        check_vma=False,
    )
```

profile of v0, /device:TPU:0, one launch (start us, length us, event | category | flops | bytes accessed | tf_op | source)
XLA Modules:
  0.0 422.1 jit_solution(1724845972538885632)
XLA Ops:
  0.7 1.6 copy-done
  2.2 1.4 fusion.10
  3.9 1.3 collective-permute-start.3
  5.3 1.3 collective-permute-start.1
  6.6 3.0 collective-permute-start.2
  9.6 5.5 %collective-permute-start = (bf16[1,64,256]{2,1,0:T(8,128)(2,1)S(1)}, bf16[1,64,256]{2,1,0:T(8,128)(2,1)S(1)}, u32[]{:S(2)}, u32[]{:S(2)}) collective-permute-start(bf16[1,64,256]{2,1,0:T(8,128)(2,1)S(1)} %bitcast.279), channel_id=1, source_target_pairs={{0,2},{2,4},{4,6},{6,8},{8,10},{10,12},{12,14},{14,16},{16,18},{18... | collective-permute-start | bytes 98312 | tf_op jit(solution)/shard_map/ppermute | solution.py:14
  18.0 4.3 %compare_select_fusion.2 = (s32[256,1]{0,1:T(1,128)S(1)}, s32[256,1]{0,1:T(1,128)S(1)}) fusion(s32[]{:T(128)} %bitcast.43, s32[]{:T(128)} %bitcast.44, s32[]{:T(128)} %bitcast.45, s32[]{:T(128)} %bitcast.46, s32[]{:T(128)} %bitcast.47, s32[]{:T(128)} %bitcast.49, s32[]{:T(128)} %bitcast.48, s32[256,1]{0,1:T(1,128)S(1)} %bitcast.344), kind=kLoop, calls=%fused_computation.128 | loop fusion | flops 3840 | bytes 3100 | tf_op jit(solution)/shard_map/jit(_take)/gather | solution.py:60
  22.4 5.5 %compare_and_fusion.1 = (pred[256]{0:T(512)(128)(4,1)S(1)}, s32[256]{0:T(256)S(1)}) fusion(pred[256]{0:T(512)(128)(4,1)S(1)} %get-tuple-element.36, pred[256]{0:T(512)(128)(4,1)S(1)} %get-tuple-element.35, pred[256]{0:T(512)(128)(4,1)S(1)} %get-tuple-element.34, pred[256]{0:T(512)(128)(4,1)S(1)} %get-tuple-element.33, ...), kind=kLoop, calls=%fused_computation.137 | loop fusion | flops 6400 | bytes 5668 | tf_op jit(solution)/shard_map/jit(_take)/and | solution.py:72
  28.4 39.8 %all_gather.12 = bf16[64,512]{0,1:T(8,128)(2,1)S(1)} all-gather(bf16[64,32]{0,1:T(8,128)(2,1)S(1)} %convolution_convert_fusion.1), channel_id=1, replica_groups=mesh['wide'=16,'narrow'=2] {'wide'}, dimensions={1}, use_global_device_ids=true | all-gather | bytes 69632 | tf_op jit(solution)/shard_map/all_gather | solution.py:71
  68.4 1.3 collective-permute-start.7
  69.7 1.3 collective-permute-start.5
  71.0 3.0 collective-permute-start.6
  74.0 4.3 %collective-permute-start.4 = (bf16[1,64,256]{2,1,0:T(8,128)(2,1)S(1)}, bf16[1,64,256]{2,1,0:T(8,128)(2,1)S(1)}, u32[]{:S(2)}, u32[]{:S(2)}) collective-permute-start(bf16[1,64,256]{2,1,0:T(8,128)(2,1)S(1)} %bitcast.282), channel_id=1, source_target_pairs={{0,2},{2,4},{4,6},{6,8},{8,10},{10,12},{12,14},{14,16},{16,18},{18... | collective-permute-start | bytes 98312 | tf_op jit(solution)/shard_map/ppermute | solution.py:14
  79.9 2.1 fusion.19
  82.4 1.3 collective-permute-start.11
  83.7 1.3 collective-permute-start.9
  85.0 3.0 collective-permute-start.10
  88.0 4.9 %collective-permute-start.8 = (bf16[1,64,256]{2,1,0:T(8,128)(2,1)S(1)}, bf16[1,64,256]{2,1,0:T(8,128)(2,1)S(1)}, u32[]{:S(2)}, u32[]{:S(2)}) collective-permute-start(bf16[1,64,256]{2,1,0:T(8,128)(2,1)S(1)} %bitcast.281), channel_id=1, source_target_pairs={{0,2},{2,4},{4,6},{6,8},{8,10},{10,12},{12,14},{14,16},{16,18},{18... | collective-permute-start | bytes 98312 | tf_op jit(solution)/shard_map/ppermute | solution.py:14
  92.9 3.4 psum.42
  96.2 38.8 %all_gather.13 = bf16[64,512]{0,1:T(8,128)(2,1)S(1)} all-gather(bf16[64,32]{0,1:T(8,128)(2,1)S(1)} %psum.42), channel_id=1, replica_groups=mesh['wide'=16,'narrow'=2] {'wide'}, dimensions={1}, use_global_device_ids=true | all-gather | bytes 69632 | tf_op jit(solution)/shard_map/all_gather | solution.py:80
  136.3 1.3 collective-permute-start.15
  137.6 1.3 collective-permute-start.13
  138.9 3.0 collective-permute-start.14
  142.0 4.3 %collective-permute-start.12 = (bf16[1,64,256]{2,1,0:T(8,128)(2,1)S(1)}, bf16[1,64,256]{2,1,0:T(8,128)(2,1)S(1)}, u32[]{:S(2)}, u32[]{:S(2)}) collective-permute-start(bf16[1,64,256]{2,1,0:T(8,128)(2,1)S(1)} %bitcast.286), channel_id=1, source_target_pairs={{0,2},{2,4},{4,6},{6,8},{8,10},{10,12},{12,14},{14,16},{16,18},{18... | collective-permute-start | bytes 98312 | tf_op jit(solution)/shard_map/ppermute | solution.py:14
  146.3 1.5 collective-permute-done.12
  148.7 1.3 collective-permute-start.19
  151.3 3.0 collective-permute-start.18
  154.3 4.9 %collective-permute-start.16 = (bf16[1,64,256]{2,1,0:T(8,128)(2,1)S(1)}, bf16[1,64,256]{2,1,0:T(8,128)(2,1)S(1)}, u32[]{:S(2)}, u32[]{:S(2)}) collective-permute-start(bf16[1,64,256]{2,1,0:T(8,128)(2,1)S(1)} %bitcast.287), channel_id=1, source_target_pairs={{0,2},{2,4},{4,6},{6,8},{8,10},{10,12},{12,14},{14,16},{16,18},{18... | collective-permute-start | bytes 98312 | tf_op jit(solution)/shard_map/ppermute | solution.py:14
  159.2 1.5 collective-permute-done.16
  161.0 41.3 %all-reduce = (f32[64]{0:T(128)S(1)}, f32[64]{0:T(128)S(1)}) all-reduce(f32[64]{0:T(128)S(1)} %get-tuple-element.27, f32[64]{0:T(128)S(1)} %get-tuple-element.26), channel_id=1, replica_groups=mesh['wide'=16,'narrow'=2] {'wide','narrow'}, use_global_device_ids=true, to_apply=%region_4.7 | all-reduce | flops 128 | bytes 1024 | tf_op jit(solution)/shard_map/psum | solution.py:41
  204.4 39.6 %all_gather.14 = bf16[64,512]{0,1:T(8,128)(2,1)S(1)} all-gather(bf16[64,32]{0,1:T(8,128)(2,1)S(1)} %convolution_convert_fusion), channel_id=1, replica_groups=mesh['wide'=16,'narrow'=2] {'wide'}, dimensions={1}, use_global_device_ids=true | all-gather | bytes 69632 | tf_op jit(solution)/shard_map/all_gather | solution.py:71
  247.7 3.0 collective-permute-start.22
  250.7 4.3 %collective-permute-start.20 = (bf16[1,64,256]{2,1,0:T(8,128)(2,1)S(1)}, bf16[1,64,256]{2,1,0:T(8,128)(2,1)S(1)}, u32[]{:S(2)}, u32[]{:S(2)}) collective-permute-start(bf16[1,64,256]{2,1,0:T(8,128)(2,1)S(1)} %bitcast.283), channel_id=1, source_target_pairs={{0,2},{2,4},{4,6},{6,8},{8,10},{10,12},{12,14},{14,16},{16,18},{18... | collective-permute-start | bytes 98312 | tf_op jit(solution)/shard_map/ppermute | solution.py:14
  256.7 2.1 fusion.22
  259.1 1.3 collective-permute-start.27
  260.4 1.3 collective-permute-start.25
  261.7 3.0 collective-permute-start.26
  264.8 4.9 %collective-permute-start.24 = (bf16[1,64,256]{2,1,0:T(8,128)(2,1)S(1)}, bf16[1,64,256]{2,1,0:T(8,128)(2,1)S(1)}, u32[]{:S(2)}, u32[]{:S(2)}) collective-permute-start(bf16[1,64,256]{2,1,0:T(8,128)(2,1)S(1)} %bitcast.280), channel_id=1, source_target_pairs={{0,2},{2,4},{4,6},{6,8},{8,10},{10,12},{12,14},{14,16},{16,18},{18... | collective-permute-start | bytes 98312 | tf_op jit(solution)/shard_map/ppermute | solution.py:14
  269.6 3.4 psum.45
  273.0 38.8 %all_gather.15 = bf16[64,512]{0,1:T(8,128)(2,1)S(1)} all-gather(bf16[64,32]{0,1:T(8,128)(2,1)S(1)} %psum.45), channel_id=1, replica_groups=mesh['wide'=16,'narrow'=2] {'wide'}, dimensions={1}, use_global_device_ids=true | all-gather | bytes 69632 | tf_op jit(solution)/shard_map/all_gather | solution.py:80
  312.9 36.9 %psum.46 = f32[64]{0:T(128)S(1)} all-reduce(f32[64]{0:T(128)S(1)} %get-tuple-element.102), channel_id=1, replica_groups=mesh['wide'=16,'narrow'=2] {'wide','narrow'}, use_global_device_ids=true, to_apply=%region_9.12 | all-reduce | flops 64 | bytes 512 | tf_op jit(solution)/shard_map/psum | solution.py:41
  352.8 3.0 collective-permute-start.30
  355.8 4.8 %collective-permute-start.28 = (bf16[1,64,256]{2,1,0:T(8,128)(2,1)S(1)}, bf16[1,64,256]{2,1,0:T(8,128)(2,1)S(1)}, u32[]{:S(2)}, u32[]{:S(2)}) collective-permute-start(bf16[1,64,256]{2,1,0:T(8,128)(2,1)S(1)} %bitcast.289), channel_id=1, source_target_pairs={{0,2},{2,4},{4,6},{6,8},{8,10},{10,12},{12,14},{14,16},{16,18},{18... | collective-permute-start | bytes 98312 | tf_op jit(solution)/shard_map/ppermute | solution.py:14
  360.7 1.5 collective-permute-done.28
  365.7 3.0 collective-permute-start.34
  368.8 5.2 %collective-permute-start.32 = (bf16[1,64,256]{2,1,0:T(8,128)(2,1)S(1)}, bf16[1,64,256]{2,1,0:T(8,128)(2,1)S(1)}, u32[]{:S(2)}, u32[]{:S(2)}) collective-permute-start(bf16[1,64,256]{2,1,0:T(8,128)(2,1)S(1)} %bitcast.290), channel_id=1, source_target_pairs={{0,2},{2,4},{4,6},{6,8},{8,10},{10,12},{12,14},{14,16},{16,18},{18... | collective-permute-start | bytes 98312 | tf_op jit(solution)/shard_map/ppermute | solution.py:14
  374.0 1.5 collective-permute-done.32
  375.8 45.4 %psum.47 = f32[64]{0:T(128)S(1)} all-reduce(f32[64]{0:T(128)S(1)} %multiply_reduce_fusion), channel_id=1, replica_groups=mesh['wide'=16,'narrow'=2] {'wide','narrow'}, use_global_device_ids=true, to_apply=%region_11.14 | all-reduce | flops 64 | bytes 512 | tf_op jit(solution)/shard_map/psum | solution.py:41
  (164 shorter events, 24.3 us)
Async XLA Ops:
  0.6 1.6 copy-start
  0.6 14.5 %copy-start.5 = (s32[2,16]{1,0:T(2,128)S(1)}, s32[2,16]{1,0:T(2,128)}, u32[]{:S(2)}) copy-start(s32[2,16]{1,0:T(2,128)} %param.15) | copy-start | bytes 388
  3.6 24.6 %copy-start.1 = (bf16[1,1,32,1024]{3,2,1,0:T(8,128)(2,1)S(1)}, bf16[1,1,32,1024]{3,2,1,0:T(8,128)(2,1)}, u32[]{:S(2)}) copy-start(bf16[1,1,32,1024]{3,2,1,0:T(8,128)(2,1)} %param.13) | copy-start | bytes 196612
  3.9 75.3 %copy-start.7 = (bf16[32,256]{1,0:T(8,128)(2,1)S(1)}, bf16[32,256]{1,0:T(8,128)(2,1)}, u32[]{:S(2)}) copy-start(bf16[32,256]{1,0:T(8,128)(2,1)} %param.14) | copy-start | bytes 49156
  3.9 24.1 %collective-permute-start.3 = (bf16[1,64,256]{2,1,0:T(8,128)(2,1)S(1)}, bf16[1,64,256]{2,1,0:T(8,128)(2,1)S(1)}, u32[]{:S(2)}, u32[]{:S(2)}) collective-permute-start(bf16[1,64,256]{2,1,0:T(8,128)(2,1)S(1)} %bitcast.275), channel_id=1, source_target_pairs={{1,0},{3,2},{5,4},{7,6},{9,8},{11,10},{13,12},{15,14},{17,16},{19,... | collective-permute-start | bytes 98312 | tf_op jit(solution)/shard_map/ppermute | solution.py:17
  5.3 22.8 %collective-permute-start.1 = (bf16[1,64,256]{2,1,0:T(8,128)(2,1)S(1)}, bf16[1,64,256]{2,1,0:T(8,128)(2,1)S(1)}, u32[]{:S(2)}, u32[]{:S(2)}) collective-permute-start(bf16[1,64,256]{2,1,0:T(8,128)(2,1)S(1)} %bitcast.276), channel_id=1, source_target_pairs={{2,0},{4,2},{6,4},{8,6},{10,8},{12,10},{14,12},{16,14},{18,16},{20... | collective-permute-start | bytes 98312 | tf_op jit(solution)/shard_map/ppermute | solution.py:17
  6.6 21.5 %collective-permute-start.2 = (bf16[1,64,256]{2,1,0:T(8,128)(2,1)S(1)}, bf16[1,64,256]{2,1,0:T(8,128)(2,1)S(1)}, u32[]{:S(2)}, u32[]{:S(2)}) collective-permute-start(bf16[1,64,256]{2,1,0:T(8,128)(2,1)S(1)} %bitcast.277), channel_id=1, source_target_pairs={{0,1},{2,3},{4,5},{6,7},{8,9},{10,11},{12,13},{14,15},{16,17},{18,... | collective-permute-start | bytes 98312 | tf_op jit(solution)/shard_map/ppermute | solution.py:14
  9.6 18.4 %collective-permute-start = (bf16[1,64,256]{2,1,0:T(8,128)(2,1)S(1)}, bf16[1,64,256]{2,1,0:T(8,128)(2,1)S(1)}, u32[]{:S(2)}, u32[]{:S(2)}) collective-permute-start(bf16[1,64,256]{2,1,0:T(8,128)(2,1)S(1)} %bitcast.279), channel_id=1, source_target_pairs={{0,2},{2,4},{4,6},{6,8},{8,10},{10,12},{12,14},{14,16},{16,18},{18... | collective-permute-start | bytes 98312 | tf_op jit(solution)/shard_map/ppermute | solution.py:14
  27.9 57.0 %copy-start.6 = (pred[256]{0:T(512)(128)(4,1)}, pred[256]{0:T(512)(128)(4,1)S(1)}, u32[]{:S(2)}) copy-start(pred[256]{0:T(512)(128)(4,1)S(1)} %get-tuple-element.41) | copy-start | bytes 772
  68.4 11.0 %collective-permute-start.7 = (bf16[1,64,256]{2,1,0:T(8,128)(2,1)S(1)}, bf16[1,64,256]{2,1,0:T(8,128)(2,1)S(1)}, u32[]{:S(2)}, u32[]{:S(2)}) collective-permute-start(bf16[1,64,256]{2,1,0:T(8,128)(2,1)S(1)} %bitcast.334), channel_id=1, source_target_pairs={{1,0},{3,2},{5,4},{7,6},{9,8},{11,10},{13,12},{15,14},{17,16},{19,... | collective-permute-start | bytes 98312 | tf_op jit(solution)/shard_map/ppermute | solution.py:17
  69.7 9.7 %collective-permute-start.5 = (bf16[1,64,256]{2,1,0:T(8,128)(2,1)S(1)}, bf16[1,64,256]{2,1,0:T(8,128)(2,1)S(1)}, u32[]{:S(2)}, u32[]{:S(2)}) collective-permute-start(bf16[1,64,256]{2,1,0:T(8,128)(2,1)S(1)} %bitcast.306), channel_id=1, source_target_pairs={{2,0},{4,2},{6,4},{8,6},{10,8},{12,10},{14,12},{16,14},{18,16},{20... | collective-permute-start | bytes 98312 | tf_op jit(solution)/shard_map/ppermute | solution.py:17
  71.0 8.4 %collective-permute-start.6 = (bf16[1,64,256]{2,1,0:T(8,128)(2,1)S(1)}, bf16[1,64,256]{2,1,0:T(8,128)(2,1)S(1)}, u32[]{:S(2)}, u32[]{:S(2)}) collective-permute-start(bf16[1,64,256]{2,1,0:T(8,128)(2,1)S(1)} %bitcast.291), channel_id=1, source_target_pairs={{0,1},{2,3},{4,5},{6,7},{8,9},{10,11},{12,13},{14,15},{16,17},{18,... | collective-permute-start | bytes 98312 | tf_op jit(solution)/shard_map/ppermute | solution.py:14
  74.0 5.9 %collective-permute-start.4 = (bf16[1,64,256]{2,1,0:T(8,128)(2,1)S(1)}, bf16[1,64,256]{2,1,0:T(8,128)(2,1)S(1)}, u32[]{:S(2)}, u32[]{:S(2)}) collective-permute-start(bf16[1,64,256]{2,1,0:T(8,128)(2,1)S(1)} %bitcast.282), channel_id=1, source_target_pairs={{0,2},{2,4},{4,6},{6,8},{8,10},{10,12},{12,14},{14,16},{16,18},{18... | collective-permute-start | bytes 98312 | tf_op jit(solution)/shard_map/ppermute | solution.py:14
  82.4 53.2 %collective-permute-start.11 = (bf16[1,64,256]{2,1,0:T(8,128)(2,1)S(1)}, bf16[1,64,256]{2,1,0:T(8,128)(2,1)S(1)}, u32[]{:S(2)}, u32[]{:S(2)}) collective-permute-start(bf16[1,64,256]{2,1,0:T(8,128)(2,1)S(1)} %bitcast.328), channel_id=1, source_target_pairs={{1,0},{3,2},{5,4},{7,6},{9,8},{11,10},{13,12},{15,14},{17,16},{19,... | collective-permute-start | bytes 98312 | tf_op jit(solution)/shard_map/ppermute | solution.py:17
  83.7 51.9 %collective-permute-start.9 = (bf16[1,64,256]{2,1,0:T(8,128)(2,1)S(1)}, bf16[1,64,256]{2,1,0:T(8,128)(2,1)S(1)}, u32[]{:S(2)}, u32[]{:S(2)}) collective-permute-start(bf16[1,64,256]{2,1,0:T(8,128)(2,1)S(1)} %bitcast.300), channel_id=1, source_target_pairs={{2,0},{4,2},{6,4},{8,6},{10,8},{12,10},{14,12},{16,14},{18,16},{20... | collective-permute-start | bytes 98312 | tf_op jit(solution)/shard_map/ppermute | solution.py:17
  85.0 50.6 %collective-permute-start.10 = (bf16[1,64,256]{2,1,0:T(8,128)(2,1)S(1)}, bf16[1,64,256]{2,1,0:T(8,128)(2,1)S(1)}, u32[]{:S(2)}, u32[]{:S(2)}) collective-permute-start(bf16[1,64,256]{2,1,0:T(8,128)(2,1)S(1)} %bitcast.285), channel_id=1, source_target_pairs={{0,1},{2,3},{4,5},{6,7},{8,9},{10,11},{12,13},{14,15},{16,17},{18,... | collective-permute-start | bytes 98312 | tf_op jit(solution)/shard_map/ppermute | solution.py:14
  88.0 47.6 %collective-permute-start.8 = (bf16[1,64,256]{2,1,0:T(8,128)(2,1)S(1)}, bf16[1,64,256]{2,1,0:T(8,128)(2,1)S(1)}, u32[]{:S(2)}, u32[]{:S(2)}) collective-permute-start(bf16[1,64,256]{2,1,0:T(8,128)(2,1)S(1)} %bitcast.281), channel_id=1, source_target_pairs={{0,2},{2,4},{4,6},{6,8},{8,10},{10,12},{12,14},{14,16},{16,18},{18... | collective-permute-start | bytes 98312 | tf_op jit(solution)/shard_map/ppermute | solution.py:14
  136.3 9.9 %collective-permute-start.15 = (bf16[1,64,256]{2,1,0:T(8,128)(2,1)S(1)}, bf16[1,64,256]{2,1,0:T(8,128)(2,1)S(1)}, u32[]{:S(2)}, u32[]{:S(2)}) collective-permute-start(bf16[1,64,256]{2,1,0:T(8,128)(2,1)S(1)} %bitcast.340), channel_id=1, source_target_pairs={{1,0},{3,2},{5,4},{7,6},{9,8},{11,10},{13,12},{15,14},{17,16},{19,... | collective-permute-start | bytes 98312 | tf_op jit(solution)/shard_map/ppermute | solution.py:17
  137.6 8.6 %collective-permute-start.13 = (bf16[1,64,256]{2,1,0:T(8,128)(2,1)S(1)}, bf16[1,64,256]{2,1,0:T(8,128)(2,1)S(1)}, u32[]{:S(2)}, u32[]{:S(2)}) collective-permute-start(bf16[1,64,256]{2,1,0:T(8,128)(2,1)S(1)} %bitcast.323), channel_id=1, source_target_pairs={{2,0},{4,2},{6,4},{8,6},{10,8},{12,10},{14,12},{16,14},{18,16},{20... | collective-permute-start | bytes 98312 | tf_op jit(solution)/shard_map/ppermute | solution.py:17
  138.9 7.3 %collective-permute-start.14 = (bf16[1,64,256]{2,1,0:T(8,128)(2,1)S(1)}, bf16[1,64,256]{2,1,0:T(8,128)(2,1)S(1)}, u32[]{:S(2)}, u32[]{:S(2)}) collective-permute-start(bf16[1,64,256]{2,1,0:T(8,128)(2,1)S(1)} %bitcast.301), channel_id=1, source_target_pairs={{0,1},{2,3},{4,5},{6,7},{8,9},{10,11},{12,13},{14,15},{16,17},{18,... | collective-permute-start | bytes 98312 | tf_op jit(solution)/shard_map/ppermute | solution.py:14
  142.0 5.9 %collective-permute-start.12 = (bf16[1,64,256]{2,1,0:T(8,128)(2,1)S(1)}, bf16[1,64,256]{2,1,0:T(8,128)(2,1)S(1)}, u32[]{:S(2)}, u32[]{:S(2)}) collective-permute-start(bf16[1,64,256]{2,1,0:T(8,128)(2,1)S(1)} %bitcast.286), channel_id=1, source_target_pairs={{0,2},{2,4},{4,6},{6,8},{8,10},{10,12},{12,14},{14,16},{16,18},{18... | collective-permute-start | bytes 98312 | tf_op jit(solution)/shard_map/ppermute | solution.py:14
  148.7 10.5 %collective-permute-start.19 = (bf16[1,64,256]{2,1,0:T(8,128)(2,1)S(1)}, bf16[1,64,256]{2,1,0:T(8,128)(2,1)S(1)}, u32[]{:S(2)}, u32[]{:S(2)}) collective-permute-start(bf16[1,64,256]{2,1,0:T(8,128)(2,1)S(1)} %bitcast.341), channel_id=1, source_target_pairs={{1,0},{3,2},{5,4},{7,6},{9,8},{11,10},{13,12},{15,14},{17,16},{19,... | collective-permute-start | bytes 98312 | tf_op jit(solution)/shard_map/ppermute | solution.py:17
  150.0 9.2 %collective-permute-start.17 = (bf16[1,64,256]{2,1,0:T(8,128)(2,1)S(1)}, bf16[1,64,256]{2,1,0:T(8,128)(2,1)S(1)}, u32[]{:S(2)}, u32[]{:S(2)}) collective-permute-start(bf16[1,64,256]{2,1,0:T(8,128)(2,1)S(1)} %bitcast.324), channel_id=1, source_target_pairs={{2,0},{4,2},{6,4},{8,6},{10,8},{12,10},{14,12},{16,14},{18,16},{20... | collective-permute-start | bytes 98312 | tf_op jit(solution)/shard_map/ppermute | solution.py:17
  151.3 7.9 %collective-permute-start.18 = (bf16[1,64,256]{2,1,0:T(8,128)(2,1)S(1)}, bf16[1,64,256]{2,1,0:T(8,128)(2,1)S(1)}, u32[]{:S(2)}, u32[]{:S(2)}) collective-permute-start(bf16[1,64,256]{2,1,0:T(8,128)(2,1)S(1)} %bitcast.302), channel_id=1, source_target_pairs={{0,1},{2,3},{4,5},{6,7},{8,9},{10,11},{12,13},{14,15},{16,17},{18,... | collective-permute-start | bytes 98312 | tf_op jit(solution)/shard_map/ppermute | solution.py:14
  154.3 6.4 %collective-permute-start.16 = (bf16[1,64,256]{2,1,0:T(8,128)(2,1)S(1)}, bf16[1,64,256]{2,1,0:T(8,128)(2,1)S(1)}, u32[]{:S(2)}, u32[]{:S(2)}) collective-permute-start(bf16[1,64,256]{2,1,0:T(8,128)(2,1)S(1)} %bitcast.287), channel_id=1, source_target_pairs={{0,2},{2,4},{4,6},{6,8},{8,10},{10,12},{12,14},{14,16},{16,18},{18... | collective-permute-start | bytes 98312 | tf_op jit(solution)/shard_map/ppermute | solution.py:14
  202.3 0.5 copy-start.8
  202.8 0.5 copy-start.3
  245.1 10.9 %collective-permute-start.23 = (bf16[1,64,256]{2,1,0:T(8,128)(2,1)S(1)}, bf16[1,64,256]{2,1,0:T(8,128)(2,1)S(1)}, u32[]{:S(2)}, u32[]{:S(2)}) collective-permute-start(bf16[1,64,256]{2,1,0:T(8,128)(2,1)S(1)} %bitcast.337), channel_id=1, source_target_pairs={{1,0},{3,2},{5,4},{7,6},{9,8},{11,10},{13,12},{15,14},{17,16},{19,... | collective-permute-start | bytes 98312 | tf_op jit(solution)/shard_map/ppermute | solution.py:17
  246.4 9.6 %collective-permute-start.21 = (bf16[1,64,256]{2,1,0:T(8,128)(2,1)S(1)}, bf16[1,64,256]{2,1,0:T(8,128)(2,1)S(1)}, u32[]{:S(2)}, u32[]{:S(2)}) collective-permute-start(bf16[1,64,256]{2,1,0:T(8,128)(2,1)S(1)} %bitcast.314), channel_id=1, source_target_pairs={{2,0},{4,2},{6,4},{8,6},{10,8},{12,10},{14,12},{16,14},{18,16},{20... | collective-permute-start | bytes 98312 | tf_op jit(solution)/shard_map/ppermute | solution.py:17
  247.7 8.3 %collective-permute-start.22 = (bf16[1,64,256]{2,1,0:T(8,128)(2,1)S(1)}, bf16[1,64,256]{2,1,0:T(8,128)(2,1)S(1)}, u32[]{:S(2)}, u32[]{:S(2)}) collective-permute-start(bf16[1,64,256]{2,1,0:T(8,128)(2,1)S(1)} %bitcast.294), channel_id=1, source_target_pairs={{0,1},{2,3},{4,5},{6,7},{8,9},{10,11},{12,13},{14,15},{16,17},{18,... | collective-permute-start | bytes 98312 | tf_op jit(solution)/shard_map/ppermute | solution.py:14
  250.7 5.9 %collective-permute-start.20 = (bf16[1,64,256]{2,1,0:T(8,128)(2,1)S(1)}, bf16[1,64,256]{2,1,0:T(8,128)(2,1)S(1)}, u32[]{:S(2)}, u32[]{:S(2)}) collective-permute-start(bf16[1,64,256]{2,1,0:T(8,128)(2,1)S(1)} %bitcast.283), channel_id=1, source_target_pairs={{0,2},{2,4},{4,6},{6,8},{8,10},{10,12},{12,14},{14,16},{16,18},{18... | collective-permute-start | bytes 98312 | tf_op jit(solution)/shard_map/ppermute | solution.py:14
  256.7 55.8 %copy-start.2 = (bf16[1,1,32,1024]{3,2,1,0:T(8,128)(2,1)S(1)}, bf16[1,1,32,1024]{3,2,1,0:T(8,128)(2,1)}, u32[]{:S(2)}) copy-start(bf16[1,1,32,1024]{3,2,1,0:T(8,128)(2,1)} %param.13) | copy-start | bytes 196612
  258.8 91.0 %copy-start.9 = (f32[64]{0:T(128)S(1)}, f32[64]{0:T(128)}, u32[]{:S(2)}) copy-start(f32[64]{0:T(128)} %copy-done.8) | copy-start | bytes 772
  259.1 53.2 %collective-permute-start.27 = (bf16[1,64,256]{2,1,0:T(8,128)(2,1)S(1)}, bf16[1,64,256]{2,1,0:T(8,128)(2,1)S(1)}, u32[]{:S(2)}, u32[]{:S(2)}) collective-permute-start(bf16[1,64,256]{2,1,0:T(8,128)(2,1)S(1)} %bitcast.325), channel_id=1, source_target_pairs={{1,0},{3,2},{5,4},{7,6},{9,8},{11,10},{13,12},{15,14},{17,16},{19,... | collective-permute-start | bytes 98312 | tf_op jit(solution)/shard_map/ppermute | solution.py:17
  260.4 51.9 %collective-permute-start.25 = (bf16[1,64,256]{2,1,0:T(8,128)(2,1)S(1)}, bf16[1,64,256]{2,1,0:T(8,128)(2,1)S(1)}, u32[]{:S(2)}, u32[]{:S(2)}) collective-permute-start(bf16[1,64,256]{2,1,0:T(8,128)(2,1)S(1)} %bitcast.299), channel_id=1, source_target_pairs={{2,0},{4,2},{6,4},{8,6},{10,8},{12,10},{14,12},{16,14},{18,16},{20... | collective-permute-start | bytes 98312 | tf_op jit(solution)/shard_map/ppermute | solution.py:17
  261.7 50.6 %collective-permute-start.26 = (bf16[1,64,256]{2,1,0:T(8,128)(2,1)S(1)}, bf16[1,64,256]{2,1,0:T(8,128)(2,1)S(1)}, u32[]{:S(2)}, u32[]{:S(2)}) collective-permute-start(bf16[1,64,256]{2,1,0:T(8,128)(2,1)S(1)} %bitcast.284), channel_id=1, source_target_pairs={{0,1},{2,3},{4,5},{6,7},{8,9},{10,11},{12,13},{14,15},{16,17},{18,... | collective-permute-start | bytes 98312 | tf_op jit(solution)/shard_map/ppermute | solution.py:14
  264.8 47.6 %collective-permute-start.24 = (bf16[1,64,256]{2,1,0:T(8,128)(2,1)S(1)}, bf16[1,64,256]{2,1,0:T(8,128)(2,1)S(1)}, u32[]{:S(2)}, u32[]{:S(2)}) collective-permute-start(bf16[1,64,256]{2,1,0:T(8,128)(2,1)S(1)} %bitcast.280), channel_id=1, source_target_pairs={{0,2},{2,4},{4,6},{6,8},{8,10},{10,12},{12,14},{14,16},{16,18},{18... | collective-permute-start | bytes 98312 | tf_op jit(solution)/shard_map/ppermute | solution.py:14
  350.2 10.5 %collective-permute-start.31 = (bf16[1,64,256]{2,1,0:T(8,128)(2,1)S(1)}, bf16[1,64,256]{2,1,0:T(8,128)(2,1)S(1)}, u32[]{:S(2)}, u32[]{:S(2)}) collective-permute-start(bf16[1,64,256]{2,1,0:T(8,128)(2,1)S(1)} %bitcast.342), channel_id=1, source_target_pairs={{1,0},{3,2},{5,4},{7,6},{9,8},{11,10},{13,12},{15,14},{17,16},{19,... | collective-permute-start | bytes 98312 | tf_op jit(solution)/shard_map/ppermute | solution.py:17
  351.5 9.2 %collective-permute-start.29 = (bf16[1,64,256]{2,1,0:T(8,128)(2,1)S(1)}, bf16[1,64,256]{2,1,0:T(8,128)(2,1)S(1)}, u32[]{:S(2)}, u32[]{:S(2)}) collective-permute-start(bf16[1,64,256]{2,1,0:T(8,128)(2,1)S(1)} %bitcast.326), channel_id=1, source_target_pairs={{2,0},{4,2},{6,4},{8,6},{10,8},{12,10},{14,12},{16,14},{18,16},{20... | collective-permute-start | bytes 98312 | tf_op jit(solution)/shard_map/ppermute | solution.py:17
  352.8 7.9 %collective-permute-start.30 = (bf16[1,64,256]{2,1,0:T(8,128)(2,1)S(1)}, bf16[1,64,256]{2,1,0:T(8,128)(2,1)S(1)}, u32[]{:S(2)}, u32[]{:S(2)}) collective-permute-start(bf16[1,64,256]{2,1,0:T(8,128)(2,1)S(1)} %bitcast.304), channel_id=1, source_target_pairs={{0,1},{2,3},{4,5},{6,7},{8,9},{10,11},{12,13},{14,15},{16,17},{18,... | collective-permute-start | bytes 98312 | tf_op jit(solution)/shard_map/ppermute | solution.py:14
  355.8 6.4 %collective-permute-start.28 = (bf16[1,64,256]{2,1,0:T(8,128)(2,1)S(1)}, bf16[1,64,256]{2,1,0:T(8,128)(2,1)S(1)}, u32[]{:S(2)}, u32[]{:S(2)}) collective-permute-start(bf16[1,64,256]{2,1,0:T(8,128)(2,1)S(1)} %bitcast.289), channel_id=1, source_target_pairs={{0,2},{2,4},{4,6},{6,8},{8,10},{10,12},{12,14},{14,16},{16,18},{18... | collective-permute-start | bytes 98312 | tf_op jit(solution)/shard_map/ppermute | solution.py:14
  362.8 58.5 %copy-start.4 = (f32[64]{0:T(128)S(1)}, f32[64]{0:T(128)}, u32[]{:S(2)}) copy-start(f32[64]{0:T(128)} %copy-done.3) | copy-start | bytes 772
  363.1 10.8 %collective-permute-start.35 = (bf16[1,64,256]{2,1,0:T(8,128)(2,1)S(1)}, bf16[1,64,256]{2,1,0:T(8,128)(2,1)S(1)}, u32[]{:S(2)}, u32[]{:S(2)}) collective-permute-start(bf16[1,64,256]{2,1,0:T(8,128)(2,1)S(1)} %bitcast.343), channel_id=1, source_target_pairs={{1,0},{3,2},{5,4},{7,6},{9,8},{11,10},{13,12},{15,14},{17,16},{19,... | collective-permute-start | bytes 98312 | tf_op jit(solution)/shard_map/ppermute | solution.py:17
  364.4 9.5 %collective-permute-start.33 = (bf16[1,64,256]{2,1,0:T(8,128)(2,1)S(1)}, bf16[1,64,256]{2,1,0:T(8,128)(2,1)S(1)}, u32[]{:S(2)}, u32[]{:S(2)}) collective-permute-start(bf16[1,64,256]{2,1,0:T(8,128)(2,1)S(1)} %bitcast.327), channel_id=1, source_target_pairs={{2,0},{4,2},{6,4},{8,6},{10,8},{12,10},{14,12},{16,14},{18,16},{20... | collective-permute-start | bytes 98312 | tf_op jit(solution)/shard_map/ppermute | solution.py:17
  365.7 8.2 %collective-permute-start.34 = (bf16[1,64,256]{2,1,0:T(8,128)(2,1)S(1)}, bf16[1,64,256]{2,1,0:T(8,128)(2,1)S(1)}, u32[]{:S(2)}, u32[]{:S(2)}) collective-permute-start(bf16[1,64,256]{2,1,0:T(8,128)(2,1)S(1)} %bitcast.305), channel_id=1, source_target_pairs={{0,1},{2,3},{4,5},{6,7},{8,9},{10,11},{12,13},{14,15},{16,17},{18,... | collective-permute-start | bytes 98312 | tf_op jit(solution)/shard_map/ppermute | solution.py:14
  368.8 6.8 %collective-permute-start.32 = (bf16[1,64,256]{2,1,0:T(8,128)(2,1)S(1)}, bf16[1,64,256]{2,1,0:T(8,128)(2,1)S(1)}, u32[]{:S(2)}, u32[]{:S(2)}) collective-permute-start(bf16[1,64,256]{2,1,0:T(8,128)(2,1)S(1)} %bitcast.290), channel_id=1, source_target_pairs={{0,2},{2,4},{4,6},{6,8},{8,10},{10,12},{12,14},{14,16},{16,18},{18... | collective-permute-start | bytes 98312 | tf_op jit(solution)/shard_map/ppermute | solution.py:14
where the time goes:
time: 424 us; the launch traced here: 422 us
  blocking collectives  287 us (68%)
  starting transfers between devices  93.3 us (22%)
  other arithmetic  11.9 us (3%)
  local copies, waits for them, and re-layouts  9.71 us (2%)
  matrix products  9.47 us (2%)
  waiting for transfers between devices  7.37 us (2%)
    psum x3, blocking collectives, load_sums(): return lax.psum(jnp.sum(left * right, axis=1), ('wide', 'narrow'))  124 us
    all_gather x2, blocking collectives, coarse_term(): padded = lax.all_gather(weights, 'wide', axis=1, tiled=True)  79.3 us
    all_gather x2, blocking collectives, coarse_term(): coarse_values = lax.all_gather(block_values, 'wide', axis=1, tiled=True)  77.5 us
    ppermute x18, starting transfers between devices, extended(): lax.ppermute(lax.slice_in_dim(block, block.shape[dim] - width, None, axis...  70.1 us
    ppermute x18, starting transfers between devices, extended(): lax.ppermute(lax.slice_in_dim(block, 0, width, axis=dim), axis, backward)  23.3 us
  transfers between devices with their start and end apart: 36, of which 6 were waited for; matrix products, arithmetic and copies ran while one was open for 4% of the time, Pallas kernels for 0%

commit v1 on v0

v1 whole, which is shorter than its diff:
```python
import functools

import jax
import jax.numpy as jnp
from jax import lax
from jax.experimental import pallas as pl
from jax.experimental.pallas import tpu as pltpu
from jax.sharding import PartitionSpec as P

MESH = pl.DeviceIdType.MESH
ITERS = 2
FACES = 4
OPPOSITE = (1, 0, 3, 2)
F32 = jnp.float32
BF16 = jnp.bfloat16


def mm(left, right):
    return jnp.dot(left, right, preferred_element_type=F32)


def mm_nt(left, right):
    return lax.dot_general(left, right, (((1,), (1,)), ((), ())), preferred_element_type=F32)


def mm_tn(left, right):
    return mm(left.T.astype(BF16), right)


def kernel(
    rows, cols, loads_hbm, flex_hbm, dirichlet_hbm, modes_hbm, inverse_hbm, counts_ref,
    mult_ref, resid_ref,
    loads, flex, dirichlet, modes, inverse, near_modes, weight_table, pick_table,
    weight_box, value_box, sum_box, out_face, in_face, moved, r_f, d_f, g_f, z_f, gz_f, x_f,
    load_sem, face_send, face_recv, setup_send, setup_recv, bulk_send, bulk_recv,
):
    total = rows * cols
    i = lax.axis_index("wide")
    j = lax.axis_index("narrow")
    me = i * cols + j
    cases = loads.shape[0]
    face = loads.shape[1] // FACES
    slots = modes.shape[0]
    half = slots // 2
    block_rows, column_width = inverse.shape[1], inverse.shape[2]
    block_half = block_rows // 2
    order = cols * column_width

    exists = (i > 0, i < rows - 1, j > 0, j < cols - 1)
    across = ((i - 1, j), (i + 1, j), (i, j - 1), (i, j + 1))
    have = [jnp.where(e, 1.0, 0.0).astype(F32) for e in exists]
    scale = [1.0 + h for h in have]

    def device(k):
        target = lax.rem(me + k, total)
        return (target // cols, lax.rem(target, cols))

    barrier = pltpu.get_barrier_semaphore()

    @pl.loop(1, total)
    def _(k):
        pl.semaphore_signal(barrier, inc=1, device_id=device(k), device_id_type=MESH)

    def fetch(source, target, number):
        copy = pltpu.make_async_copy(source, target, load_sem.at[number])
        copy.start()
        return copy

    get_loads = fetch(loads_hbm, loads, 0)
    get_flex = [
        fetch(flex_hbm.at[:, pl.ds(f * face, face)], flex.at[f], 1 + f) for f in range(FACES)
    ]
    get_modes = fetch(modes_hbm, modes, 9)
    get_inverse = fetch(inverse_hbm, inverse.at[j], 10)
    get_dirichlet = [
        fetch(dirichlet_hbm.at[:, pl.ds(f * face, face)], dirichlet.at[f], 5 + f)
        for f in range(FACES)
    ]

    for f in range(FACES):
        @pl.when(jnp.logical_not(exists[f]))
        def _():
            in_face[:, f] = jnp.zeros((in_face.shape[0], cases, face), BF16)
            near_modes[f] = jnp.zeros((slots, face), BF16)

    def face_copy(use, f):
        return pltpu.make_async_remote_copy(
            src_ref=out_face.at[use, f],
            dst_ref=in_face.at[use, OPPOSITE[f]],
            send_sem=face_send.at[use, f],
            recv_sem=face_recv.at[use, OPPOSITE[f]],
            device_id=across[f],
            device_id_type=MESH,
        )

    def face_start(use, f):
        @pl.when(exists[f])
        def _():
            face_copy(use, f).start()

    def face_wait(use, f):
        @pl.when(exists[f])
        def _():
            pltpu.make_async_remote_copy(
                src_ref=out_face.at[use, f],
                dst_ref=in_face.at[use, f],
                send_sem=face_send.at[use, f],
                recv_sem=face_recv.at[use, f],
                device_id=across[f],
                device_id_type=MESH,
            ).wait_recv()

    def modes_copy(f, slot):
        return pltpu.make_async_remote_copy(
            src_ref=modes.at[:, pl.ds(f * face, face)],
            dst_ref=near_modes.at[slot],
            send_sem=setup_send.at[f],
            recv_sem=setup_recv.at[slot],
            device_id=across[f],
            device_id_type=MESH,
        )

    def bulk(box, number, slot, target):
        return pltpu.make_async_remote_copy(
            src_ref=box.at[slot],
            dst_ref=box.at[slot],
            send_sem=bulk_send.at[number],
            recv_sem=bulk_recv.at[number],
            device_id=target,
            device_id_type=MESH,
        )

    def to_all(box, number):
        @pl.loop(1, total)
        def _(k):
            bulk(box, number, me, device(k)).start()

    def to_column(box, number):
        @pl.loop(1, rows)
        def _(k):
            bulk(box, number, i, (lax.rem(i + k, rows), j)).start()

    def to_row(box, number):
        @pl.loop(1, cols)
        def _(k):
            bulk(box, number, j, (i, lax.rem(j + k, cols))).start()

    def all_of(box, number):
        most = box.shape[0] - 1
        return pltpu.make_async_remote_copy(
            src_ref=box.at[pl.ds(0, most)],
            dst_ref=box.at[pl.ds(0, most)],
            send_sem=bulk_send.at[number],
            recv_sem=bulk_recv.at[number],
            device_id=device(1),
            device_id_type=MESH,
        )

    def row_sum(field):
        part = field[:, : face // 2] + field[:, face // 2 :]
        while part.shape[1] > 128:
            part = part[:, : part.shape[1] // 2] + part[:, part.shape[1] // 2 :]
        part = jnp.concatenate([part, jnp.zeros((128 - cases, 128), F32)], axis=0)
        return jnp.sum(part.T, axis=0, keepdims=True)

    def as_column(row):
        part = jnp.broadcast_to(row, (128, 128)).T[:cases]
        return jnp.concatenate([part] * (face // 128), axis=1)

    def share_sum(number, row):
        box = sum_box.at[number]
        box[pl.ds(me, 1)] = row[None]
        to_all(box, number)

    def take_sum(number):
        box = sum_box.at[number]
        all_of(box, number).wait_recv()
        return jnp.sum(box[...], axis=0)

    sums = 2 * ITERS

    def pack(values):
        low = values.shape[0] // 2
        return jnp.concatenate([values[:low], values[low:]], axis=1)

    get_loads.wait()
    for f in range(FACES):
        get_flex[f].wait()
        out_face[0, f] = mm(loads[...], flex[f]).astype(BF16)
        if f == 0:
            pl.semaphore_wait(barrier, total - 1)
        face_start(0, f)

    get_modes.wait()
    get_inverse.wait()
    for f in range(FACES):
        @pl.when(exists[f])
        def _():
            modes_copy(f, OPPOSITE[f]).start()
    to_row(inverse, sums)

    counts = counts_ref[...].astype(F32).astype(BF16)
    tile = min(total * half, 512)
    chunk = min(column_width, 256)
    all_of(inverse, sums).wait_recv()

    @pl.loop(0, total * half // tile)
    def _(tile_index):
        at = pl.multiple_of(tile_index * tile, tile)
        lane = at + lax.broadcasted_iota(jnp.int32, (rows, tile), 1)
        row_of = lane // (half * cols)
        down = lax.broadcasted_iota(jnp.int32, (rows, tile), 0)
        begin = mm(counts, jnp.where(down < row_of, 1.0, 0.0).astype(BF16))
        count = mm(counts, jnp.where(down == row_of, 1.0, 0.0).astype(BF16))
        lane_c = at + lax.broadcasted_iota(jnp.int32, (cols, tile), 1)
        column_of = lax.rem(lane_c // half, cols)
        which = lax.broadcasted_iota(jnp.int32, (cols, tile), 0)
        mine = which == column_of
        begin = begin + (column_of * column_width).astype(F32)
        begin = jnp.sum(jnp.where(mine, begin, 0.0), axis=0, keepdims=True)
        count = jnp.sum(jnp.where(mine, count, 0.0), axis=0, keepdims=True)
        lane_1 = at + lax.broadcasted_iota(jnp.int32, (1, tile), 1)
        rank = lax.rem(lane_1, half).astype(F32)
        for h in range(2):
            slot = rank + float(h * half)
            number = jnp.where(slot < count, begin + slot, -1.0)
            gathered = jnp.zeros((block_rows, tile), F32)
            for column in range(cols):
                def add(c, carry, column=column, number=number):
                    first = pl.multiple_of(c * chunk, chunk)
                    down_b = lax.broadcasted_iota(jnp.int32, (chunk, tile), 0)
                    b = (down_b + (column * column_width + first)).astype(F32)
                    hot = jnp.where(b == number, 1.0, 0.0).astype(BF16)
                    return carry + mm(inverse[column, :, pl.ds(first, chunk)], hot)
                gathered = lax.fori_loop(0, column_width // chunk, add, gathered)
            block_down = lax.broadcasted_iota(jnp.int32, (block_rows, tile), 0)
            own = (block_down + i * block_rows).astype(F32)
            weight_table[pl.ds(h * block_rows, block_rows), pl.ds(at, tile)] = gathered.astype(BF16)
            weight_table[pl.ds((2 + h) * block_rows, block_rows), pl.ds(at, tile)] = jnp.where(
                own == number, 1.0, 0.0
            ).astype(BF16)

    count_f = counts_ref[...].astype(F32)
    down = lax.broadcasted_iota(jnp.int32, (cols, rows), 0)
    along = lax.broadcasted_iota(jnp.int32, (cols, rows), 1)

    def pick(row, column):
        begin = jnp.sum(
            jnp.where((down == column) & (along < row), count_f, 0.0), keepdims=True
        )
        count = jnp.sum(
            jnp.where((down == column) & (along == row), count_f, 0.0), keepdims=True
        )
        return begin + (column * column_width).astype(F32), count

    for s, (row, column) in enumerate(((i, j),) + across):
        begin, count = pick(row, column)
        rank = lax.broadcasted_iota(jnp.int32, (slots, 1), 0).astype(F32)
        number = jnp.where(rank < count, begin + rank, -1.0)
        lane = lax.broadcasted_iota(jnp.int32, (slots, rows * block_half), 1)
        for h in range(2):
            a = (lane // block_half) * block_rows + lax.rem(lane, block_half) + h * block_half
            pick_table[h, pl.ds(s * slots, slots)] = jnp.where(
                a.astype(F32) == number, 1.0, 0.0
            ).astype(BF16)

    for f in range(FACES):
        face_wait(0, f)
        r_f[f] = out_face[0, f].astype(F32) - in_face[0, f].astype(F32)

    def precondition(turn, use):
        w_box, v_box = weight_box.at[turn], value_box.at[turn]
        w_number, v_number = sums + 1 + 2 * turn, sums + 2 + 2 * turn
        weights = jnp.zeros((slots, cases), F32)
        for f in range(FACES):
            rounded = r_f[f].astype(BF16)
            weights = weights + mm_nt(modes[:, f * face : (f + 1) * face], rounded)
            moved[:, f * face : (f + 1) * face] = (rounded.astype(F32) * scale[f]).astype(BF16)
        w_box[pl.ds(me, 1)] = pack(weights).astype(BF16)[None]
        to_all(w_box, w_number)

        total_f = jnp.zeros((cases, face), F32)
        for f in range(FACES):
            if turn == 0:
                get_dirichlet[f].wait()
            smoothed = mm(moved[...], dirichlet[f]).astype(BF16)
            out_face[use, f] = smoothed
            face_start(use, f)
            total_f = total_f + (r_f[f] * scale[f]) * smoothed.astype(F32)
        row = row_sum(total_f)

        all_of(w_box, w_number).wait_recv()
        out = mm(weight_table[...], w_box[...].reshape(total * half, 2 * cases))
        b = block_rows
        values = (out[:b, :cases] + out[b : 2 * b, cases:]).astype(BF16)
        own = out[2 * b : 3 * b, :cases] + out[3 * b :, cases:]
        v_box[pl.ds(i, 1)] = pack(values.astype(F32)).astype(BF16)[None]
        to_column(v_box, v_number)
        inner = jnp.sum(values.astype(F32) * own, axis=0, keepdims=True)
        inner = jnp.concatenate([inner, jnp.zeros((1, 128 - cases), F32)], axis=1)
        row = row + inner * jnp.where(j == 0, 1.0, 0.0)
        share_sum(2 * turn, row)

        for f in range(FACES):
            face_wait(use, f)
            local = out_face[use, f].astype(F32) - in_face[use, f].astype(F32)
            z_f[f] = local
            gz_f[f] = -local * have[f]
        if turn == 0:
            for f in range(FACES):
                @pl.when(exists[f])
                def _():
                    modes_copy(f, f).wait_recv()

        all_of(v_box, v_number).wait_recv()
        flat = v_box[...].reshape(rows * block_half, 2 * cases)
        picked = mm(pick_table[0], flat)[:, :cases] + mm(pick_table[1], flat)[:, cases:]
        own_picked = picked[:slots].T.astype(BF16)
        for f in range(FACES):
            z_f[f] = z_f[f] + mm(own_picked, modes[:, f * face : (f + 1) * face])
            gz_f[f] = gz_f[f] + mm_tn(picked[(1 + f) * slots : (2 + f) * slots], near_modes[f])

    precondition(0, 1)
    energy = None
    use = 2
    for turn in range(ITERS):
        if turn == 0:
            for f in range(FACES):
                d_f[f] = z_f[f]
                g_f[f] = gz_f[f]
        else:
            fresh = take_sum(2 * turn)
            beta = as_column(fresh / energy)
            energy = fresh
            for f in range(FACES):
                d_f[f] = z_f[f] + beta * d_f[f]
                g_f[f] = gz_f[f] + beta * g_f[f]
        for f in range(FACES):
            moved[:, f * face : (f + 1) * face] = (
                d_f[f].astype(BF16).astype(F32) - g_f[f].astype(BF16).astype(F32)
            ).astype(BF16)
        total_f = jnp.zeros((cases, face), F32)
        for f in range(FACES):
            image = mm(moved[...], flex[f]).astype(BF16)
            out_face[use, f] = image
            face_start(use, f)
            total_f = total_f + (d_f[f] - g_f[f]) * image.astype(F32)
        share_sum(2 * turn + 1, row_sum(total_f))
        if turn == 0:
            energy = take_sum(0)
        for f in range(FACES):
            face_wait(use, f)
        step = as_column(energy / take_sum(2 * turn + 1))
        for f in range(FACES):
            image = out_face[use, f].astype(F32) - in_face[use, f].astype(F32)
            residual = r_f[f] - step * image
            advance = step * d_f[f]
            if turn > 0:
                advance = x_f[f] + advance
            if turn + 1 < ITERS:
                r_f[f] = residual
                x_f[f] = advance
            else:
                mult_ref[:, f * face : (f + 1) * face] = advance.astype(BF16)
                resid_ref[:, f * face : (f + 1) * face] = residual.astype(BF16)
        use += 1
        if turn + 1 < ITERS:
            precondition(turn + 1, use)
            use += 1

    for f in range(FACES):
        @pl.when(exists[f])
        def _():
            modes_copy(f, OPPOSITE[f]).wait_send()
            for use in range(2 * ITERS + 1):
                face_copy(use, f).wait_send()
    for number in range(sums):
        all_of(sum_box.at[number], number).wait_send()
    all_of(inverse, sums).wait_send()
    for turn in range(ITERS):
        all_of(weight_box.at[turn], sums + 1 + 2 * turn).wait_send()
        all_of(value_box.at[turn], sums + 2 + 2 * turn).wait_send()


def shards(rows, cols, loads, flexibility, dirichlet, modes, coarse_inverse, mode_counts):
    _, _, cases, width = loads.shape
    slots = modes.shape[2]
    block_rows, column_width = coarse_inverse.shape
    total = rows * cols
    face = width // FACES
    uses = 2 * ITERS + 1
    bulks = 2 * ITERS + 1 + 2 * ITERS
    anywhere = pl.BlockSpec(memory_space=pl.ANY)
    inside = pl.BlockSpec(memory_space=pltpu.VMEM)
    field = pltpu.VMEM((FACES, cases, face), F32)
    dma = pltpu.SemaphoreType.DMA
    mult, resid = pl.pallas_call(
        functools.partial(kernel, rows, cols),
        out_shape=[jax.ShapeDtypeStruct((cases, width), BF16)] * 2,
        in_specs=[anywhere] * 5 + [inside],
        out_specs=[inside] * 2,
        scratch_shapes=[
            pltpu.VMEM((cases, width), BF16),
            pltpu.VMEM((FACES, width, face), BF16),
            pltpu.VMEM((FACES, width, face), BF16),
            pltpu.VMEM((slots, width), BF16),
            pltpu.VMEM((cols, block_rows, column_width), BF16),
            pltpu.VMEM((FACES, slots, face), BF16),
            pltpu.VMEM((4 * block_rows, total * slots // 2), BF16),
            pltpu.VMEM((2, (1 + FACES) * slots, rows * block_rows // 2), BF16),
            pltpu.VMEM((ITERS, total, slots // 2, 2 * cases), BF16),
            pltpu.VMEM((ITERS, rows, block_rows // 2, 2 * cases), BF16),
            pltpu.VMEM((2 * ITERS, total, 1, 128), F32),
            pltpu.VMEM((uses, FACES, cases, face), BF16),
            pltpu.VMEM((uses, FACES, cases, face), BF16),
            pltpu.VMEM((cases, width), BF16),
            field, field, field, field, field, field,
            dma((11,)),
            dma((uses, FACES)),
            dma((uses, FACES)),
            dma((FACES,)),
            dma((FACES,)),
            dma((bulks,)),
            dma((bulks,)),
        ],
        compiler_params=pltpu.CompilerParams(
            collective_id=0, has_side_effects=True, vmem_limit_bytes=40 * 1024 * 1024
        ),
    )(
        loads.reshape(cases, width),
        flexibility.reshape(width, width),
        dirichlet.reshape(width, width),
        modes.reshape(slots, width),
        coarse_inverse,
        mode_counts,
    )
    return mult[None, None], resid[None, None]


def solution(mesh):
    return jax.shard_map(
        functools.partial(shards, mesh.shape["wide"], mesh.shape["narrow"]),
        mesh=mesh,
        in_specs=(
            P("wide", "narrow", None, None),
            P("wide", "narrow", None, None),
            P("wide", "narrow", None, None),
            P("wide", "narrow", None, None),
            P("wide", "narrow"),
            P(),
        ),
        out_specs=(P("wide", "narrow", None, None), P("wide", "narrow", None, None)),
        check_vma=False,
    )
```

time: 424 us -> 53.5 us (0.13)
  blocking collectives: 287 us -> 0 us
  starting transfers between devices: 93.3 us -> 0 us
  Pallas kernels: 0 us -> 44.9 us
  other arithmetic: 11.9 us -> 0 us
  matrix products: 9.47 us -> 0 us
  waiting for transfers between devices: 7.37 us -> 0 us
    all_gather x4 -> x0, blocking collectives: 157 us -> none  [the longest x2 79.3 us: coarse_term(): padded = lax.all_gather(weights, 'wide', axis=1, tiled=True)]
    psum x5 -> x0, blocking collectives: 130 us -> none  [the longest x3 124 us: load_sums(): return lax.psum(jnp.sum(left * right, axis=1), ('wide', 'narrow'))]
    ppermute x36 -> x0, starting transfers between devices: 93.3 us -> none  [the longest x18 70.1 us: extended(): lax.ppermute(lax.slice_in_dim(block, block.shape[dim] - width, None, axis...]
    pallas_call x0 -> x1, Pallas kernels: none -> 44.9 us  [shards(): pl.pallas_call(functools.partial(kernel, rows, cols), out_shape=[jax.Shap...]
    dot_general x11 -> x0, matrix products: 9.47 us -> none  [the longest x2 4.18 us: precondition(): jnp.dot(inner, precond_block, preferred_element_type=jnp.float32)]
    ppermute x36 -> x0, waiting for transfers between devices: 7.37 us -> none  [the longest x18 7.32 us: extended(): lax.ppermute(lax.slice_in_dim(block, block.shape[dim] - width, None, axis...]
    and x2 -> x0, other arithmetic: 5.56 us -> none  [the longest x1 5.55 us: coarse_term(): column_values = jnp.take(padded, slot_index, axis=1)]
    unnamed x56 -> x14, local copies, waits for them, and re-layouts: 2.83 us -> 7.63 us
  transfers between devices with their start and end apart: 36 -> 0, of which waited for: 6 -> 0; matrix products, arithmetic and copies ran while one was open for 4% -> 0% of each run, Pallas kernels for 0% -> 0%
where the time goes in v1:
time: 53.5 us; the launch traced here: 53.2 us
  Pallas kernels  44.9 us (84%)
  local copies, waits for them, and re-layouts  7.63 us (14%)
  between operations  0.65 us (1%)
    pallas_call x1, Pallas kernels, shards(): pl.pallas_call(functools.partial(kernel, rows, cols), out_shape=[jax.Shap...  44.9 us
    unnamed x14, local copies, waits for them, and re-layouts  7.63 us

profile of v1, /device:TPU:0, one launch (start us, length us, event | category | flops | bytes accessed | tf_op | source)
XLA Modules:
  0.0 53.2 jit_solution(11550365936425441468)
XLA Ops:
  0.6 0.0 copy-start
  0.6 1.6 %copy-done = bf16[1,1,1024,1024]{3,2,1,0:T(8,128)(2,1)S(1)} copy-done((bf16[1,1,1024,1024]{3,2,1,0:T(8,128)(2,1)S(1)}, bf16[1,1,1024,1024]{3,2,1,0:T(8,128)(2,1)}, u32[]{:S(2)}) %copy-start) | copy-done | bytes 2097176
  2.2 0.0 copy-start.1
  2.2 1.6 %copy-done.1 = bf16[1,1,1024,1024]{3,2,1,0:T(8,128)(2,1)S(1)} copy-done((bf16[1,1,1024,1024]{3,2,1,0:T(8,128)(2,1)S(1)}, bf16[1,1,1024,1024]{3,2,1,0:T(8,128)(2,1)}, u32[]{:S(2)}) %copy-start.1) | copy-done | bytes 2097176
  3.8 0.0 copy-start.2
  3.8 0.9 %copy-done.2 = bf16[1,1,64,1024]{3,2,1,0:T(8,128)(2,1)S(1)} copy-done((bf16[1,1,64,1024]{3,2,1,0:T(8,128)(2,1)S(1)}, bf16[1,1,64,1024]{3,2,1,0:T(8,128)(2,1)}, u32[]{:S(2)}) %copy-start.2) | copy-done | bytes 131096
  4.7 0.0 copy-start.3
  4.7 0.8 %copy-done.3 = bf16[1,1,32,1024]{3,2,1,0:T(8,128)(2,1)S(1)} copy-done((bf16[1,1,32,1024]{3,2,1,0:T(8,128)(2,1)S(1)}, bf16[1,1,32,1024]{3,2,1,0:T(8,128)(2,1)}, u32[]{:S(2)}) %copy-start.3) | copy-done | bytes 65560
  5.6 0.0 copy-start.4
  5.6 0.7 %copy-done.4 = bf16[32,256]{1,0:T(8,128)(2,1)S(1)} copy-done((bf16[32,256]{1,0:T(8,128)(2,1)S(1)}, bf16[32,256]{1,0:T(8,128)(2,1)}, u32[]{:S(2)}) %copy-start.4) | copy-done | bytes 16408
  6.3 0.0 copy-start.5
  6.3 0.7 %copy-done.5 = s32[2,16]{1,0:T(2,128)S(1)} copy-done((s32[2,16]{1,0:T(2,128)S(1)}, s32[2,16]{1,0:T(2,128)}, u32[]{:S(2)}) %copy-start.5) | copy-done | bytes 152
  7.0 44.9 %shard_map.77 = (bf16[64,1024]{1,0:T(8,128)(2,1)S(1)}, bf16[64,1024]{1,0:T(8,128)(2,1)S(1)}) custom-call(bf16[64,1024]{1,0:T(8,128)(2,1)S(1)} %bitcast.8, bf16[1024,1024]{1,0:T(8,128)(2,1)S(1)} %bitcast.6, bf16[1024,1024]{1,0:T(8,128)(2,1)S(1)} %bitcast.7, bf16[32,1024]{1,0:T(8,128)(2,1)S(1)} %bitcast.11, bf16[32,256]{1,0:T(8,128)(2,1)S(1)} %copy-done.4, ...), custom_call_target="tpu_custom_call" | custom-call | tf_op jit(solution)/shard_map/pallas_call | solution.py:397
  51.9 0.7 %copy.10 = bf16[1,1,64,1024]{3,2,1,0:T(8,128)(2,1)} copy(bf16[1,1,64,1024]{3,2,1,0:T(8,128)(2,1)S(1)} %bitcast.10) | data formatting | bytes 262144
  52.6 0.7 %copy.11 = bf16[1,1,64,1024]{3,2,1,0:T(8,128)(2,1)} copy(bf16[1,1,64,1024]{3,2,1,0:T(8,128)(2,1)S(1)} %bitcast.9) | data formatting | bytes 262144
Async XLA Ops:
  0.6 1.6 %copy-start = (bf16[1,1,1024,1024]{3,2,1,0:T(8,128)(2,1)S(1)}, bf16[1,1,1024,1024]{3,2,1,0:T(8,128)(2,1)}, u32[]{:S(2)}) copy-start(bf16[1,1,1024,1024]{3,2,1,0:T(8,128)(2,1)} %param.7) | copy-start | bytes 6291460
  2.2 1.6 %copy-start.1 = (bf16[1,1,1024,1024]{3,2,1,0:T(8,128)(2,1)S(1)}, bf16[1,1,1024,1024]{3,2,1,0:T(8,128)(2,1)}, u32[]{:S(2)}) copy-start(bf16[1,1,1024,1024]{3,2,1,0:T(8,128)(2,1)} %param.8) | copy-start | bytes 6291460
  3.8 0.9 %copy-start.2 = (bf16[1,1,64,1024]{3,2,1,0:T(8,128)(2,1)S(1)}, bf16[1,1,64,1024]{3,2,1,0:T(8,128)(2,1)}, u32[]{:S(2)}) copy-start(bf16[1,1,64,1024]{3,2,1,0:T(8,128)(2,1)} %param.6) | copy-start | bytes 393220
  4.7 0.8 %copy-start.3 = (bf16[1,1,32,1024]{3,2,1,0:T(8,128)(2,1)S(1)}, bf16[1,1,32,1024]{3,2,1,0:T(8,128)(2,1)}, u32[]{:S(2)}) copy-start(bf16[1,1,32,1024]{3,2,1,0:T(8,128)(2,1)} %param.9) | copy-start | bytes 196612
  5.6 0.7 %copy-start.4 = (bf16[32,256]{1,0:T(8,128)(2,1)S(1)}, bf16[32,256]{1,0:T(8,128)(2,1)}, u32[]{:S(2)}) copy-start(bf16[32,256]{1,0:T(8,128)(2,1)} %inverse_hbm.1) | copy-start | bytes 49156
  6.3 0.7 %copy-start.5 = (s32[2,16]{1,0:T(2,128)S(1)}, s32[2,16]{1,0:T(2,128)}, u32[]{:S(2)}) copy-start(s32[2,16]{1,0:T(2,128)} %counts_ref.1) | copy-start | bytes 388

commit v2 on v1

--- a/solution.py
+++ b/solution.py
@@ -8,6 +8,7 @@
 from jax.sharding import PartitionSpec as P
 
 MESH = pl.DeviceIdType.MESH
+LOGICAL = pl.DeviceIdType.LOGICAL
 ITERS = 2
 FACES = 4
 OPPOSITE = (1, 0, 3, 2)
@@ -52,14 +53,21 @@
     scale = [1.0 + h for h in have]
 
     def device(k):
-        target = lax.rem(me + k, total)
-        return (target // cols, lax.rem(target, cols))
+        return lax.rem(me + k, total)
+
+    def repeat(last, body):
+        if last <= 64:
+            for k in range(1, last):
+                body(k)
+        else:
+            pl.loop(1, last)(body)
 
     barrier = pltpu.get_barrier_semaphore()
 
-    @pl.loop(1, total)
-    def _(k):
-        pl.semaphore_signal(barrier, inc=1, device_id=device(k), device_id_type=MESH)
+    def greet(k):
+        pl.semaphore_signal(barrier, inc=1, device_id=device(k), device_id_type=LOGICAL)
+
+    repeat(total, greet)
 
     def fetch(source, target, number):
         copy = pltpu.make_async_copy(source, target, load_sem.at[number])
@@ -127,23 +135,17 @@
             send_sem=bulk_send.at[number],
             recv_sem=bulk_recv.at[number],
             device_id=target,
-            device_id_type=MESH,
+            device_id_type=LOGICAL,
         )
 
     def to_all(box, number):
-        @pl.loop(1, total)
-        def _(k):
-            bulk(box, number, me, device(k)).start()
+        repeat(total, lambda k: bulk(box, number, me, device(k)).start())
 
     def to_column(box, number):
-        @pl.loop(1, rows)
-        def _(k):
-            bulk(box, number, i, (lax.rem(i + k, rows), j)).start()
+        repeat(rows, lambda k: bulk(box, number, i, device(k * cols)).start())
 
     def to_row(box, number):
-        @pl.loop(1, cols)
-        def _(k):
-            bulk(box, number, j, (i, lax.rem(j + k, cols))).start()
+        repeat(cols, lambda k: bulk(box, number, j, i * cols + lax.rem(j + k, cols)).start())
 
     def all_of(box, number):
         most = box.shape[0] - 1
@@ -153,7 +155,7 @@
             send_sem=bulk_send.at[number],
             recv_sem=bulk_recv.at[number],
             device_id=device(1),
-            device_id_type=MESH,
+            device_id_type=LOGICAL,
         )
 
     def row_sum(field):
@@ -299,7 +301,8 @@
         inner = jnp.sum(values.astype(F32) * own, axis=0, keepdims=True)
         inner = jnp.concatenate([inner, jnp.zeros((1, 128 - cases), F32)], axis=1)
         row = row + inner * jnp.where(j == 0, 1.0, 0.0)
-        share_sum(2 * turn, row)
+        if turn > 0:
+            share_sum(2 * turn, jnp.concatenate([row, row], axis=1))
 
         for f in range(FACES):
             face_wait(use, f)
@@ -319,8 +322,9 @@
         for f in range(FACES):
             z_f[f] = z_f[f] + mm(own_picked, modes[:, f * face : (f + 1) * face])
             gz_f[f] = gz_f[f] + mm_tn(picked[(1 + f) * slots : (2 + f) * slots], near_modes[f])
-
-    precondition(0, 1)
+        return row
+
+    first_energy = precondition(0, 1)
     energy = None
     use = 2
     for turn in range(ITERS):
@@ -329,7 +333,7 @@
                 d_f[f] = z_f[f]
                 g_f[f] = gz_f[f]
         else:
-            fresh = take_sum(2 * turn)
+            fresh = take_sum(2 * turn)[:, :128]
             beta = as_column(fresh / energy)
             energy = fresh
             for f in range(FACES):
@@ -345,12 +349,14 @@
             out_face[use, f] = image
             face_start(use, f)
             total_f = total_f + (d_f[f] - g_f[f]) * image.astype(F32)
-        share_sum(2 * turn + 1, row_sum(total_f))
+        row = row_sum(total_f)
+        share_sum(2 * turn + 1, jnp.concatenate([row, first_energy], axis=1))
+        for f in range(FACES):
+            face_wait(use, f)
+        both = take_sum(2 * turn + 1)
         if turn == 0:
-            energy = take_sum(0)
-        for f in range(FACES):
-            face_wait(use, f)
-        step = as_column(energy / take_sum(2 * turn + 1))
+            energy = both[:, 128:]
+        step = as_column(energy / both[:, :128])
         for f in range(FACES):
             image = out_face[use, f].astype(F32) - in_face[use, f].astype(F32)
             residual = r_f[f] - step * image
@@ -374,7 +380,7 @@
             modes_copy(f, OPPOSITE[f]).wait_send()
             for use in range(2 * ITERS + 1):
                 face_copy(use, f).wait_send()
-    for number in range(sums):
+    for number in range(1, sums):
         all_of(sum_box.at[number], number).wait_send()
     all_of(inverse, sums).wait_send()
     for turn in range(ITERS):
@@ -410,7 +416,7 @@
             pltpu.VMEM((2, (1 + FACES) * slots, rows * block_rows // 2), BF16),
             pltpu.VMEM((ITERS, total, slots // 2, 2 * cases), BF16),
             pltpu.VMEM((ITERS, rows, block_rows // 2, 2 * cases), BF16),
-            pltpu.VMEM((2 * ITERS, total, 1, 128), F32),
+            pltpu.VMEM((2 * ITERS, total, 1, 256), F32),
             pltpu.VMEM((uses, FACES, cases, face), BF16),
             pltpu.VMEM((uses, FACES, cases, face), BF16),
             pltpu.VMEM((cases, width), BF16),
@@ -424,7 +430,7 @@
             dma((bulks,)),
         ],
         compiler_params=pltpu.CompilerParams(
-            collective_id=0, has_side_effects=True, vmem_limit_bytes=40 * 1024 * 1024
+            collective_id=0, has_side_effects=True, vmem_limit_bytes=62 * 1024 * 1024
         ),
     )(
         loads.reshape(cases, width),

time: 53.5 us -> 50.3 us (0.940)
  local copies, waits for them, and re-layouts: 7.63 us -> 3.14 us
  Pallas kernels: 44.9 us -> 46.3 us
    unnamed x14 -> x2, local copies, waits for them, and re-layouts: 7.63 us -> 3.14 us
    pallas_call x1, Pallas kernels: 44.9 us -> 46.3 us  [shards(): pl.pallas_call(functools.partial(kernel, rows, cols), out_shape=[jax.Shap...]
where the time goes in v2:
time: 50.3 us; the launch traced here: 50.1 us
  Pallas kernels  46.3 us (92%)
  local copies, waits for them, and re-layouts  3.14 us (6%)
  between operations  0.64 us (1%)
    pallas_call x1, Pallas kernels, shards(): pl.pallas_call(functools.partial(kernel, rows, cols), out_shape=[jax.Shap...  46.3 us
    unnamed x2, local copies, waits for them, and re-layouts  3.14 us

profile of v2, /device:TPU:0, one launch (start us, length us, event | category | flops | bytes accessed | tf_op | source)
XLA Modules:
  0.0 50.1 jit_solution(12837271300284053586)
XLA Ops:
  0.6 46.3 %shard_map.77 = (bf16[64,1024]{1,0:T(8,128)(2,1)}, bf16[64,1024]{1,0:T(8,128)(2,1)}) custom-call(bf16[64,1024]{1,0:T(8,128)(2,1)} %bitcast.8, bf16[1024,1024]{1,0:T(8,128)(2,1)} %bitcast.6, bf16[1024,1024]{1,0:T(8,128)(2,1)} %bitcast.7, bf16[32,1024]{1,0:T(8,128)(2,1)} %bitcast.11, bf16[32,256]{1,0:T(8,128)(2,1)} %inverse_hbm.1, s32[2,16]{1,0:T(2,128)} %counts_ref.1), custom_call_target="tpu_custom_call" | custom-call | tf_op jit(solution)/shard_map/pallas_call | solution.py:403
  47.0 1.6 %copy.10 = bf16[1,1,64,1024]{3,2,1,0:T(8,128)(2,1)} copy(bf16[1,1,64,1024]{3,2,1,0:T(8,128)(2,1)} %bitcast.10) | data formatting | bytes 262144
  48.5 1.6 %copy.11 = bf16[1,1,64,1024]{3,2,1,0:T(8,128)(2,1)} copy(bf16[1,1,64,1024]{3,2,1,0:T(8,128)(2,1)} %bitcast.9) | data formatting | bytes 262144

commit v3 on v2

--- a/solution.py
+++ b/solution.py
@@ -29,10 +29,10 @@
 
 
 def kernel(
-    rows, cols, loads_hbm, flex_hbm, dirichlet_hbm, modes_hbm, inverse_hbm, counts_ref,
+    rows, cols, direct, loads_hbm, flex_hbm, dirichlet_hbm, modes_hbm, inverse_hbm, counts_hbm,
     mult_ref, resid_ref,
-    loads, flex, dirichlet, modes, inverse, near_modes, weight_table, pick_table,
-    weight_box, value_box, sum_box, out_face, in_face, moved, r_f, d_f, g_f, z_f, gz_f, x_f,
+    loads, flex, dirichlet, modes, inverse, counts_ref, near_modes, weight_table, pick_table,
+    weight_box, value_box, own_box, sum_box, out_face, in_face, moved, r_f, d_f, g_f, z_f, gz_f, x_f,
     load_sem, face_send, face_recv, setup_send, setup_recv, bulk_send, bulk_recv,
 ):
     total = rows * cols
@@ -79,7 +79,8 @@
         fetch(flex_hbm.at[:, pl.ds(f * face, face)], flex.at[f], 1 + f) for f in range(FACES)
     ]
     get_modes = fetch(modes_hbm, modes, 9)
-    get_inverse = fetch(inverse_hbm, inverse.at[j], 10)
+    get_inverse = fetch(inverse_hbm, inverse.at[i if direct else j], 10)
+    get_counts = fetch(counts_hbm, counts_ref, 11)
     get_dirichlet = [
         fetch(dirichlet_hbm.at[:, pl.ds(f * face, face)], dirichlet.at[f], 5 + f)
         for f in range(FACES)
@@ -185,6 +186,13 @@
         low = values.shape[0] // 2
         return jnp.concatenate([values[:low], values[low:]], axis=1)
 
+    def unpack(values):
+        values = values.astype(F32)
+        return jnp.concatenate([values[:, :cases], values[:, cases:]], axis=0)
+
+    def widen(row):
+        return jnp.concatenate([row, jnp.zeros((1, 128 - cases), F32)], axis=1)
+
     get_loads.wait()
     for f in range(FACES):
         get_flex[f].wait()
@@ -199,48 +207,81 @@
         @pl.when(exists[f])
         def _():
             modes_copy(f, OPPOSITE[f]).start()
-    to_row(inverse, sums)
-
+    if direct:
+        to_column(inverse, sums)
+    else:
+        to_row(inverse, sums)
+
+    get_counts.wait()
     counts = counts_ref[...].astype(F32).astype(BF16)
-    tile = min(total * half, 512)
-    chunk = min(column_width, 256)
-    all_of(inverse, sums).wait_recv()
-
-    @pl.loop(0, total * half // tile)
-    def _(tile_index):
-        at = pl.multiple_of(tile_index * tile, tile)
-        lane = at + lax.broadcasted_iota(jnp.int32, (rows, tile), 1)
-        row_of = lane // (half * cols)
-        down = lax.broadcasted_iota(jnp.int32, (rows, tile), 0)
+
+    def direct_table():
+        span = rows * half
+        lane = lax.broadcasted_iota(jnp.int32, (rows, span), 1)
+        down = lax.broadcasted_iota(jnp.int32, (rows, span), 0)
+        row_of = lane // half
         begin = mm(counts, jnp.where(down < row_of, 1.0, 0.0).astype(BF16))
         count = mm(counts, jnp.where(down == row_of, 1.0, 0.0).astype(BF16))
-        lane_c = at + lax.broadcasted_iota(jnp.int32, (cols, tile), 1)
-        column_of = lax.rem(lane_c // half, cols)
-        which = lax.broadcasted_iota(jnp.int32, (cols, tile), 0)
-        mine = which == column_of
-        begin = begin + (column_of * column_width).astype(F32)
+        mine = lax.broadcasted_iota(jnp.int32, (cols, span), 0) == j
         begin = jnp.sum(jnp.where(mine, begin, 0.0), axis=0, keepdims=True)
         count = jnp.sum(jnp.where(mine, count, 0.0), axis=0, keepdims=True)
-        lane_1 = at + lax.broadcasted_iota(jnp.int32, (1, tile), 1)
-        rank = lax.rem(lane_1, half).astype(F32)
+        rank = lax.rem(lax.broadcasted_iota(jnp.int32, (1, span), 1), half).astype(F32)
+        b = lax.broadcasted_iota(jnp.int32, (column_width, span), 0).astype(F32)
         for h in range(2):
             slot = rank + float(h * half)
             number = jnp.where(slot < count, begin + slot, -1.0)
-            gathered = jnp.zeros((block_rows, tile), F32)
-            for column in range(cols):
-                def add(c, carry, column=column, number=number):
-                    first = pl.multiple_of(c * chunk, chunk)
-                    down_b = lax.broadcasted_iota(jnp.int32, (chunk, tile), 0)
-                    b = (down_b + (column * column_width + first)).astype(F32)
-                    hot = jnp.where(b == number, 1.0, 0.0).astype(BF16)
-                    return carry + mm(inverse[column, :, pl.ds(first, chunk)], hot)
-                gathered = lax.fori_loop(0, column_width // chunk, add, gathered)
-            block_down = lax.broadcasted_iota(jnp.int32, (block_rows, tile), 0)
-            own = (block_down + i * block_rows).astype(F32)
-            weight_table[pl.ds(h * block_rows, block_rows), pl.ds(at, tile)] = gathered.astype(BF16)
-            weight_table[pl.ds((2 + h) * block_rows, block_rows), pl.ds(at, tile)] = jnp.where(
-                own == number, 1.0, 0.0
+            weight_table[pl.ds(order, column_width), pl.ds(h * span, span)] = jnp.where(
+                b == number, 1.0, 0.0
             ).astype(BF16)
+        all_of(inverse, sums).wait_recv()
+        hot = weight_table[pl.ds(order, column_width), :]
+        weight_table[pl.ds(0, order), :] = mm(
+            inverse[...].reshape(order, column_width), hot
+        ).astype(BF16)
+
+    def spread_table():
+        all_of(inverse, sums).wait_recv()
+        tile = min(total * half, 512)
+        chunk = min(column_width, 256)
+
+        @pl.loop(0, total * half // tile)
+        def _(tile_index):
+            at = pl.multiple_of(tile_index * tile, tile)
+            lane = at + lax.broadcasted_iota(jnp.int32, (rows, tile), 1)
+            row_of = lane // (half * cols)
+            down = lax.broadcasted_iota(jnp.int32, (rows, tile), 0)
+            begin = mm(counts, jnp.where(down < row_of, 1.0, 0.0).astype(BF16))
+            count = mm(counts, jnp.where(down == row_of, 1.0, 0.0).astype(BF16))
+            lane_c = at + lax.broadcasted_iota(jnp.int32, (cols, tile), 1)
+            column_of = lax.rem(lane_c // half, cols)
+            which = lax.broadcasted_iota(jnp.int32, (cols, tile), 0)
+            mine = which == column_of
+            begin = begin + (column_of * column_width).astype(F32)
+            begin = jnp.sum(jnp.where(mine, begin, 0.0), axis=0, keepdims=True)
+            count = jnp.sum(jnp.where(mine, count, 0.0), axis=0, keepdims=True)
+            lane_1 = at + lax.broadcasted_iota(jnp.int32, (1, tile), 1)
+            rank = lax.rem(lane_1, half).astype(F32)
+            for h in range(2):
+                slot = rank + float(h * half)
+                number = jnp.where(slot < count, begin + slot, -1.0)
+                gathered = jnp.zeros((block_rows, tile), F32)
+                for column in range(cols):
+                    def add(c, carry, column=column, number=number):
+                        first = pl.multiple_of(c * chunk, chunk)
+                        down_b = lax.broadcasted_iota(jnp.int32, (chunk, tile), 0)
+                        b = (down_b + (column * column_width + first)).astype(F32)
+                        hot = jnp.where(b == number, 1.0, 0.0).astype(BF16)
+                        return carry + mm(inverse[column, :, pl.ds(first, chunk)], hot)
+                    gathered = lax.fori_loop(0, column_width // chunk, add, gathered)
+                block_down = lax.broadcasted_iota(jnp.int32, (block_rows, tile), 0)
+                own = (block_down + i * block_rows).astype(F32)
+                weight_table[pl.ds(h * block_rows, block_rows), pl.ds(at, tile)] = gathered.astype(BF16)
+                weight_table[pl.ds((2 + h) * block_rows, block_rows), pl.ds(at, tile)] = jnp.where(
+                    own == number, 1.0, 0.0
+                ).astype(BF16)
+
+    if not direct:
+        spread_table()
 
     count_f = counts_ref[...].astype(F32)
     down = lax.broadcasted_iota(jnp.int32, (cols, rows), 0)
@@ -259,6 +300,12 @@
         begin, count = pick(row, column)
         rank = lax.broadcasted_iota(jnp.int32, (slots, 1), 0).astype(F32)
         number = jnp.where(rank < count, begin + rank, -1.0)
+        if direct:
+            lane = lax.broadcasted_iota(jnp.int32, (slots, order), 1)
+            pick_table[0, pl.ds(s * slots, slots)] = jnp.where(
+                lane.astype(F32) == number, 1.0, 0.0
+            ).astype(BF16)
+            continue
         lane = lax.broadcasted_iota(jnp.int32, (slots, rows * block_half), 1)
         for h in range(2):
             a = (lane // block_half) * block_rows + lax.rem(lane, block_half) + h * block_half
@@ -272,14 +319,18 @@
 
     def precondition(turn, use):
         w_box, v_box = weight_box.at[turn], value_box.at[turn]
-        w_number, v_number = sums + 1 + 2 * turn, sums + 2 + 2 * turn
+        w_number, v_number, o_number = (sums + 1 + 3 * turn + n for n in range(3))
         weights = jnp.zeros((slots, cases), F32)
         for f in range(FACES):
             rounded = r_f[f].astype(BF16)
             weights = weights + mm_nt(modes[:, f * face : (f + 1) * face], rounded)
             moved[:, f * face : (f + 1) * face] = (rounded.astype(F32) * scale[f]).astype(BF16)
-        w_box[pl.ds(me, 1)] = pack(weights).astype(BF16)[None]
-        to_all(w_box, w_number)
+        if direct:
+            w_box[pl.ds(i, 1)] = pack(weights).astype(BF16)[None]
+            to_column(w_box, w_number)
+        else:
+            w_box[pl.ds(me, 1)] = pack(weights).astype(BF16)[None]
+            to_all(w_box, w_number)
 
         total_f = jnp.zeros((cases, face), F32)
         for f in range(FACES):
@@ -291,18 +342,30 @@
             total_f = total_f + (r_f[f] * scale[f]) * smoothed.astype(F32)
         row = row_sum(total_f)
 
-        all_of(w_box, w_number).wait_recv()
-        out = mm(weight_table[...], w_box[...].reshape(total * half, 2 * cases))
-        b = block_rows
-        values = (out[:b, :cases] + out[b : 2 * b, cases:]).astype(BF16)
-        own = out[2 * b : 3 * b, :cases] + out[3 * b :, cases:]
-        v_box[pl.ds(i, 1)] = pack(values.astype(F32)).astype(BF16)[None]
-        to_column(v_box, v_number)
-        inner = jnp.sum(values.astype(F32) * own, axis=0, keepdims=True)
-        inner = jnp.concatenate([inner, jnp.zeros((1, 128 - cases), F32)], axis=1)
-        row = row + inner * jnp.where(j == 0, 1.0, 0.0)
-        if turn > 0:
-            share_sum(2 * turn, jnp.concatenate([row, row], axis=1))
+        both = jnp.concatenate([row, row], axis=1)
+        if direct:
+            if turn > 0:
+                share_sum(2 * turn, both)
+            else:
+                direct_table()
+            all_of(w_box, w_number).wait_recv()
+            out = mm(weight_table[...], unpack(w_box[...].reshape(rows * half, 2 * cases)).astype(BF16))
+            v_box[pl.ds(j, 1)] = pack(out[:order])[None]
+            own_box[turn, pl.ds(j, 1)] = pack(out[order:]).astype(BF16)[None]
+            to_row(v_box, v_number)
+            to_row(own_box.at[turn], o_number)
+        else:
+            all_of(w_box, w_number).wait_recv()
+            out = mm(weight_table[...], w_box[...].reshape(total * half, 2 * cases))
+            b = block_rows
+            values = (out[:b, :cases] + out[b : 2 * b, cases:]).astype(BF16)
+            own = out[2 * b : 3 * b, :cases] + out[3 * b :, cases:]
+            v_box[pl.ds(i, 1)] = pack(values.astype(F32)).astype(BF16)[None]
+            to_column(v_box, v_number)
+            inner = jnp.sum(values.astype(F32) * own, axis=0, keepdims=True)
+            row = row + widen(inner) * jnp.where(j == 0, 1.0, 0.0)
+            if turn > 0:
+                share_sum(2 * turn, jnp.concatenate([row, row], axis=1))
 
         for f in range(FACES):
             face_wait(use, f)
@@ -316,15 +379,23 @@
                     modes_copy(f, f).wait_recv()
 
         all_of(v_box, v_number).wait_recv()
-        flat = v_box[...].reshape(rows * block_half, 2 * cases)
-        picked = mm(pick_table[0], flat)[:, :cases] + mm(pick_table[1], flat)[:, cases:]
+        extra = jnp.zeros((1, 128), F32)
+        if direct:
+            all_of(own_box.at[turn], o_number).wait_recv()
+            values = unpack(jnp.sum(v_box[...], axis=0)).astype(BF16)
+            own = jnp.concatenate([unpack(own_box[turn, k]) for k in range(cols)], axis=0)
+            extra = widen(jnp.sum(values.astype(F32) * own, axis=0, keepdims=True))
+            picked = mm(pick_table[0], values)
+        else:
+            flat = v_box[...].reshape(rows * block_half, 2 * cases)
+            picked = mm(pick_table[0], flat)[:, :cases] + mm(pick_table[1], flat)[:, cases:]
         own_picked = picked[:slots].T.astype(BF16)
         for f in range(FACES):
             z_f[f] = z_f[f] + mm(own_picked, modes[:, f * face : (f + 1) * face])
             gz_f[f] = gz_f[f] + mm_tn(picked[(1 + f) * slots : (2 + f) * slots], near_modes[f])
-        return row
-
-    first_energy = precondition(0, 1)
+        return row, extra
+
+    first_energy, extra = precondition(0, 1)
     energy = None
     use = 2
     for turn in range(ITERS):
@@ -333,7 +404,7 @@
                 d_f[f] = z_f[f]
                 g_f[f] = gz_f[f]
         else:
-            fresh = take_sum(2 * turn)[:, :128]
+            fresh = take_sum(2 * turn)[:, :128] + extra
             beta = as_column(fresh / energy)
             energy = fresh
             for f in range(FACES):
@@ -355,7 +426,7 @@
             face_wait(use, f)
         both = take_sum(2 * turn + 1)
         if turn == 0:
-            energy = both[:, 128:]
+            energy = both[:, 128:] + extra
         step = as_column(energy / both[:, :128])
         for f in range(FACES):
             image = out_face[use, f].astype(F32) - in_face[use, f].astype(F32)
@@ -371,7 +442,7 @@
                 resid_ref[:, f * face : (f + 1) * face] = residual.astype(BF16)
         use += 1
         if turn + 1 < ITERS:
-            precondition(turn + 1, use)
+            _, extra = precondition(turn + 1, use)
             use += 1
 
     for f in range(FACES):
@@ -384,8 +455,19 @@
         all_of(sum_box.at[number], number).wait_send()
     all_of(inverse, sums).wait_send()
     for turn in range(ITERS):
-        all_of(weight_box.at[turn], sums + 1 + 2 * turn).wait_send()
-        all_of(value_box.at[turn], sums + 2 + 2 * turn).wait_send()
+        all_of(weight_box.at[turn], sums + 1 + 3 * turn).wait_send()
+        all_of(value_box.at[turn], sums + 2 + 3 * turn).wait_send()
+        if direct:
+            all_of(own_box.at[turn], sums + 3 + 3 * turn).wait_send()
+
+
+def settle(mult_in, resid_in, mult_out, resid_out, sem):
+    first = pltpu.make_async_copy(mult_in, mult_out, sem.at[0])
+    second = pltpu.make_async_copy(resid_in, resid_out, sem.at[1])
+    first.start()
+    second.start()
+    first.wait()
+    second.wait()
 
 
 def shards(rows, cols, loads, flexibility, dirichlet, modes, coarse_inverse, mode_counts):
@@ -395,33 +477,48 @@
     total = rows * cols
     face = width // FACES
     uses = 2 * ITERS + 1
-    bulks = 2 * ITERS + 1 + 2 * ITERS
+    bulks = 2 * ITERS + 1 + 3 * ITERS
+    half, order = slots // 2, cols * column_width
+    direct = order * column_width <= 1 << 20
+    if direct:
+        coarse = [
+            pltpu.VMEM((order + column_width, rows * slots), BF16),
+            pltpu.VMEM((1, (1 + FACES) * slots, order), BF16),
+            pltpu.VMEM((ITERS, rows, half, 2 * cases), BF16),
+            pltpu.VMEM((ITERS, cols, order // 2, 2 * cases), F32),
+        ]
+    else:
+        coarse = [
+            pltpu.VMEM((4 * block_rows, total * half), BF16),
+            pltpu.VMEM((2, (1 + FACES) * slots, rows * block_rows // 2), BF16),
+            pltpu.VMEM((ITERS, total, half, 2 * cases), BF16),
+            pltpu.VMEM((ITERS, rows, block_rows // 2, 2 * cases), BF16),
+        ]
     anywhere = pl.BlockSpec(memory_space=pl.ANY)
     inside = pl.BlockSpec(memory_space=pltpu.VMEM)
     field = pltpu.VMEM((FACES, cases, face), F32)
     dma = pltpu.SemaphoreType.DMA
     mult, resid = pl.pallas_call(
-        functools.partial(kernel, rows, cols),
+        functools.partial(kernel, rows, cols, direct),
         out_shape=[jax.ShapeDtypeStruct((cases, width), BF16)] * 2,
-        in_specs=[anywhere] * 5 + [inside],
+        in_specs=[anywhere] * 6,
         out_specs=[inside] * 2,
         scratch_shapes=[
             pltpu.VMEM((cases, width), BF16),
             pltpu.VMEM((FACES, width, face), BF16),
             pltpu.VMEM((FACES, width, face), BF16),
             pltpu.VMEM((slots, width), BF16),
-            pltpu.VMEM((cols, block_rows, column_width), BF16),
+            pltpu.VMEM((rows if direct else cols, block_rows, column_width), BF16),
+            pltpu.VMEM((cols, rows), jnp.int32),
             pltpu.VMEM((FACES, slots, face), BF16),
-            pltpu.VMEM((4 * block_rows, total * slots // 2), BF16),
-            pltpu.VMEM((2, (1 + FACES) * slots, rows * block_rows // 2), BF16),
-            pltpu.VMEM((ITERS, total, slots // 2, 2 * cases), BF16),
-            pltpu.VMEM((ITERS, rows, block_rows // 2, 2 * cases), BF16),
+            *coarse,
+            pltpu.VMEM((ITERS, cols, column_width // 2, 2 * cases), BF16),
             pltpu.VMEM((2 * ITERS, total, 1, 256), F32),
             pltpu.VMEM((uses, FACES, cases, face), BF16),
             pltpu.VMEM((uses, FACES, cases, face), BF16),
             pltpu.VMEM((cases, width), BF16),
             field, field, field, field, field, field,
-            dma((11,)),
+            dma((12,)),
             dma((uses, FACES)),
             dma((uses, FACES)),
             dma((FACES,)),
@@ -440,6 +537,13 @@
         coarse_inverse,
         mode_counts,
     )
+    mult, resid = pl.pallas_call(
+        settle,
+        out_shape=[jax.ShapeDtypeStruct((cases, width), BF16)] * 2,
+        in_specs=[anywhere] * 2,
+        out_specs=[anywhere] * 2,
+        scratch_shapes=[dma((2,))],
+    )(mult, resid)
     return mult[None, None], resid[None, None]
 
 

time: 50.3 us -> 49.4 us (0.982)
  local copies, waits for them, and re-layouts: 3.14 us -> 0 us
  Pallas kernels: 46.3 us -> 48.6 us
    unnamed x2 -> x0, local copies, waits for them, and re-layouts: 3.14 us -> none
    pallas_call x1 -> x2, Pallas kernels: 46.3 us -> 48.6 us  [the longest x1 39.6 us: shards(): pl.pallas_call(functools.partial(kernel, rows, cols, direct), out_shape=[...]
where the time goes in v3:
time: 49.4 us; the launch traced here: 49.3 us
  Pallas kernels  48.6 us (98%)
  between operations  0.64 us (1%)
    pallas_call x1, Pallas kernels, shards(): pl.pallas_call(functools.partial(kernel, rows, cols, direct), out_shape=[...  39.6 us
    pallas_call x1, Pallas kernels, shards(): pl.pallas_call(settle, out_shape=[jax.ShapeDtypeStruct((cases, width), BF...  9.06 us

profile of v3, /device:TPU:0, one launch (start us, length us, event | category | flops | bytes accessed | tf_op | source)
XLA Modules:
  0.0 49.3 jit_solution(4267577284876589491)
XLA Ops:
  0.6 39.6 %shard_map.77 = (bf16[64,1024]{1,0:T(8,128)(2,1)}, bf16[64,1024]{1,0:T(8,128)(2,1)}) custom-call(bf16[64,1024]{1,0:T(8,128)(2,1)} %bitcast.8, bf16[1024,1024]{1,0:T(8,128)(2,1)} %bitcast.6, bf16[1024,1024]{1,0:T(8,128)(2,1)} %bitcast.7, bf16[32,1024]{1,0:T(8,128)(2,1)} %bitcast.9, bf16[32,256]{1,0:T(8,128)(2,1)} %inverse_hbm.1, s32[2,16]{1,0:T(2,128)} %counts_hbm.1), custom_call_target="tpu_custom_call" | custom-call | tf_op jit(solution)/shard_map/pallas_call | solution.py:501
  40.2 9.1 %shard_map.78 = (bf16[64,1024]{1,0:T(8,128)(2,1)}, bf16[64,1024]{1,0:T(8,128)(2,1)}) custom-call(bf16[64,1024]{1,0:T(8,128)(2,1)} %get-tuple-element.6.mult_in, bf16[64,1024]{1,0:T(8,128)(2,1)} %get-tuple-element.7.resid_in), custom_call_target="tpu_custom_call" | custom-call | tf_op jit(solution)/shard_map/pallas_call | solution.py:540

commit v4 on v3

--- a/solution.py
+++ b/solution.py
@@ -57,17 +57,10 @@
 
     def repeat(last, body):
         if last <= 64:
-            for k in range(1, last):
+            for k in sorted(range(1, last), key=lambda k: abs(2 * k - last)):
                 body(k)
         else:
             pl.loop(1, last)(body)
-
-    barrier = pltpu.get_barrier_semaphore()
-
-    def greet(k):
-        pl.semaphore_signal(barrier, inc=1, device_id=device(k), device_id_type=LOGICAL)
-
-    repeat(total, greet)
 
     def fetch(source, target, number):
         copy = pltpu.make_async_copy(source, target, load_sem.at[number])
@@ -78,6 +71,13 @@
     get_flex = [
         fetch(flex_hbm.at[:, pl.ds(f * face, face)], flex.at[f], 1 + f) for f in range(FACES)
     ]
+    barrier = pltpu.get_barrier_semaphore()
+
+    def greet(k):
+        pl.semaphore_signal(barrier, inc=1, device_id=device(k), device_id_type=LOGICAL)
+
+    repeat(total, greet)
+
     get_modes = fetch(modes_hbm, modes, 9)
     get_inverse = fetch(inverse_hbm, inverse.at[i if direct else j], 10)
     get_counts = fetch(counts_hbm, counts_ref, 11)
@@ -461,13 +461,9 @@
             all_of(own_box.at[turn], sums + 3 + 3 * turn).wait_send()
 
 
-def settle(mult_in, resid_in, mult_out, resid_out, sem):
-    first = pltpu.make_async_copy(mult_in, mult_out, sem.at[0])
-    second = pltpu.make_async_copy(resid_in, resid_out, sem.at[1])
-    first.start()
-    second.start()
-    first.wait()
-    second.wait()
+def settle(mult_in, resid_in, mult_out, resid_out):
+    mult_out[...] = mult_in[...]
+    resid_out[...] = resid_in[...]
 
 
 def shards(rows, cols, loads, flexibility, dirichlet, modes, coarse_inverse, mode_counts):
@@ -540,9 +536,9 @@
     mult, resid = pl.pallas_call(
         settle,
         out_shape=[jax.ShapeDtypeStruct((cases, width), BF16)] * 2,
-        in_specs=[anywhere] * 2,
-        out_specs=[anywhere] * 2,
-        scratch_shapes=[dma((2,))],
+        in_specs=[inside] * 2,
+        out_specs=[inside] * 2,
+        compiler_params=pltpu.CompilerParams(vmem_limit_bytes=62 * 1024 * 1024),
     )(mult, resid)
     return mult[None, None], resid[None, None]
 

time: 49.4 us -> 42.7 us (0.86)
  Pallas kernels: 48.6 us -> 41.9 us
    pallas_call x1, Pallas kernels: 9.06 us -> 1.68 us  [shards(): pl.pallas_call(settle, out_shape=[jax.ShapeDtypeStruct((cases, width), BF...]
    pallas_call x1, Pallas kernels: 39.6 us -> 40.2 us  [shards(): pl.pallas_call(functools.partial(kernel, rows, cols, direct), out_shape=[...]
where the time goes in v4:
time: 42.7 us; the launch traced here: 42.5 us
  Pallas kernels  41.9 us (98%)
  between operations  0.64 us (1%)
    pallas_call x1, Pallas kernels, shards(): pl.pallas_call(functools.partial(kernel, rows, cols, direct), out_shape=[...  40.2 us
    pallas_call x1, Pallas kernels, shards(): pl.pallas_call(settle, out_shape=[jax.ShapeDtypeStruct((cases, width), BF...  1.68 us

profile of v4, /device:TPU:0, one launch (start us, length us, event | category | flops | bytes accessed | tf_op | source)
XLA Modules:
  0.0 42.5 jit_solution(7006661103003718324)
XLA Ops:
  0.6 40.2 %shard_map.77 = (bf16[64,1024]{1,0:T(8,128)(2,1)}, bf16[64,1024]{1,0:T(8,128)(2,1)}) custom-call(bf16[64,1024]{1,0:T(8,128)(2,1)} %bitcast.8, bf16[1024,1024]{1,0:T(8,128)(2,1)} %bitcast.6, bf16[1024,1024]{1,0:T(8,128)(2,1)} %bitcast.7, bf16[32,1024]{1,0:T(8,128)(2,1)} %bitcast.9, bf16[32,256]{1,0:T(8,128)(2,1)} %inverse_hbm.1, s32[2,16]{1,0:T(2,128)} %counts_hbm.1), custom_call_target="tpu_custom_call" | custom-call | tf_op jit(solution)/shard_map/pallas_call | solution.py:497
  40.9 1.7 %shard_map.78 = (bf16[64,1024]{1,0:T(8,128)(2,1)}, bf16[64,1024]{1,0:T(8,128)(2,1)}) custom-call(bf16[64,1024]{1,0:T(8,128)(2,1)} %get-tuple-element.6.mult_in, bf16[64,1024]{1,0:T(8,128)(2,1)} %get-tuple-element.7.resid_in), custom_call_target="tpu_custom_call" | custom-call | tf_op jit(solution)/shard_map/pallas_call | solution.py:536

commit v5 on v4

--- a/solution.py
+++ b/solution.py
@@ -12,6 +12,7 @@
 ITERS = 2
 FACES = 4
 OPPOSITE = (1, 0, 3, 2)
+PAIRS = ((0, 1), (2, 3))
 F32 = jnp.float32
 BF16 = jnp.bfloat16
 
@@ -194,12 +195,15 @@
         return jnp.concatenate([row, jnp.zeros((1, 128 - cases), F32)], axis=1)
 
     get_loads.wait()
-    for f in range(FACES):
-        get_flex[f].wait()
-        out_face[0, f] = mm(loads[...], flex[f]).astype(BF16)
-        if f == 0:
+    for pair in PAIRS:
+        for f in pair:
+            get_flex[f].wait()
+        for f in pair:
+            out_face[0, f] = mm(loads[...], flex[f]).astype(BF16)
+        if pair == PAIRS[0]:
             pl.semaphore_wait(barrier, total - 1)
-        face_start(0, f)
+        for f in pair:
+            face_start(0, f)
 
     get_modes.wait()
     get_inverse.wait()
@@ -333,13 +337,16 @@
             to_all(w_box, w_number)
 
         total_f = jnp.zeros((cases, face), F32)
-        for f in range(FACES):
-            if turn == 0:
-                get_dirichlet[f].wait()
-            smoothed = mm(moved[...], dirichlet[f]).astype(BF16)
-            out_face[use, f] = smoothed
-            face_start(use, f)
-            total_f = total_f + (r_f[f] * scale[f]) * smoothed.astype(F32)
+        for pair in PAIRS:
+            for f in pair:
+                if turn == 0:
+                    get_dirichlet[f].wait()
+            for f in pair:
+                out_face[use, f] = mm(moved[...], dirichlet[f]).astype(BF16)
+            for f in pair:
+                face_start(use, f)
+        for f in range(FACES):
+            total_f = total_f + (r_f[f] * scale[f]) * out_face[use, f].astype(F32)
         row = row_sum(total_f)
 
         both = jnp.concatenate([row, row], axis=1)
@@ -415,22 +422,25 @@
                 d_f[f].astype(BF16).astype(F32) - g_f[f].astype(BF16).astype(F32)
             ).astype(BF16)
         total_f = jnp.zeros((cases, face), F32)
-        for f in range(FACES):
-            image = mm(moved[...], flex[f]).astype(BF16)
-            out_face[use, f] = image
-            face_start(use, f)
-            total_f = total_f + (d_f[f] - g_f[f]) * image.astype(F32)
+        for pair in PAIRS:
+            for f in pair:
+                out_face[use, f] = mm(moved[...], flex[f]).astype(BF16)
+            for f in pair:
+                face_start(use, f)
+        for f in range(FACES):
+            total_f = total_f + (d_f[f] - g_f[f]) * out_face[use, f].astype(F32)
         row = row_sum(total_f)
         share_sum(2 * turn + 1, jnp.concatenate([row, first_energy], axis=1))
         for f in range(FACES):
             face_wait(use, f)
+        for f in range(FACES):
+            z_f[f] = out_face[use, f].astype(F32) - in_face[use, f].astype(F32)
         both = take_sum(2 * turn + 1)
         if turn == 0:
             energy = both[:, 128:] + extra
         step = as_column(energy / both[:, :128])
         for f in range(FACES):
-            image = out_face[use, f].astype(F32) - in_face[use, f].astype(F32)
-            residual = r_f[f] - step * image
+            residual = r_f[f] - step * z_f[f]
             advance = step * d_f[f]
             if turn > 0:
                 advance = x_f[f] + advance

time: 42.7 us -> 41 us (0.960)
  Pallas kernels: 41.9 us -> 40.2 us
    pallas_call x1, Pallas kernels: 40.2 us -> 38.6 us  [shards(): pl.pallas_call(functools.partial(kernel, rows, cols, direct), out_shape=[...]
where the time goes in v5:
time: 41 us; the launch traced here: 40.9 us
  Pallas kernels  40.2 us (98%)
  between operations  0.64 us (2%)
    pallas_call x1, Pallas kernels, shards(): pl.pallas_call(functools.partial(kernel, rows, cols, direct), out_shape=[...  38.6 us
    pallas_call x1, Pallas kernels, shards(): pl.pallas_call(settle, out_shape=[jax.ShapeDtypeStruct((cases, width), BF...  1.68 us

profile of v5, /device:TPU:0, one launch (start us, length us, event | category | flops | bytes accessed | tf_op | source)
XLA Modules:
  0.0 40.9 jit_solution(5339417849551645512)
XLA Ops:
  0.6 38.6 %shard_map.77 = (bf16[64,1024]{1,0:T(8,128)(2,1)}, bf16[64,1024]{1,0:T(8,128)(2,1)}) custom-call(bf16[64,1024]{1,0:T(8,128)(2,1)} %bitcast.8, bf16[1024,1024]{1,0:T(8,128)(2,1)} %bitcast.6, bf16[1024,1024]{1,0:T(8,128)(2,1)} %bitcast.7, bf16[32,1024]{1,0:T(8,128)(2,1)} %bitcast.9, bf16[32,256]{1,0:T(8,128)(2,1)} %inverse_hbm.1, s32[2,16]{1,0:T(2,128)} %counts_hbm.1), custom_call_target="tpu_custom_call" | custom-call | tf_op jit(solution)/shard_map/pallas_call | solution.py:507
  39.2 1.7 %shard_map.78 = (bf16[64,1024]{1,0:T(8,128)(2,1)}, bf16[64,1024]{1,0:T(8,128)(2,1)}) custom-call(bf16[64,1024]{1,0:T(8,128)(2,1)} %get-tuple-element.6.mult_in, bf16[64,1024]{1,0:T(8,128)(2,1)} %get-tuple-element.7.resid_in), custom_call_target="tpu_custom_call" | custom-call | tf_op jit(solution)/shard_map/pallas_call | solution.py:546

commit v6 on v5

--- a/solution.py
+++ b/solution.py
@@ -422,15 +422,16 @@
                 d_f[f].astype(BF16).astype(F32) - g_f[f].astype(BF16).astype(F32)
             ).astype(BF16)
         total_f = jnp.zeros((cases, face), F32)
-        for pair in PAIRS:
-            for f in pair:
-                out_face[use, f] = mm(moved[...], flex[f]).astype(BF16)
-            for f in pair:
-                face_start(use, f)
-        for f in range(FACES):
-            total_f = total_f + (d_f[f] - g_f[f]) * out_face[use, f].astype(F32)
+        for f in range(FACES):
+            image = mm(moved[...], flex[f]).astype(BF16)
+            out_face[use, f] = image
+            total_f = total_f + (d_f[f] - g_f[f]) * image.astype(F32)
         row = row_sum(total_f)
+        for f in PAIRS[0]:
+            face_start(use, f)
         share_sum(2 * turn + 1, jnp.concatenate([row, first_energy], axis=1))
+        for f in PAIRS[1]:
+            face_start(use, f)
         for f in range(FACES):
             face_wait(use, f)
         for f in range(FACES):

time: 41 us -> 40.7 us (level)
  no operation moved by 1% of the time
where the time goes in v6:
time: 40.7 us; the launch traced here: 40.5 us
  Pallas kernels  39.9 us (98%)
  between operations  0.64 us (2%)
    pallas_call x1, Pallas kernels, shards(): pl.pallas_call(functools.partial(kernel, rows, cols, direct), out_shape=[...  38.2 us
    pallas_call x1, Pallas kernels, shards(): pl.pallas_call(settle, out_shape=[jax.ShapeDtypeStruct((cases, width), BF...  1.68 us

profile of v6, /device:TPU:0, one launch (start us, length us, event | category | flops | bytes accessed | tf_op | source)
XLA Modules:
  0.0 40.5 jit_solution(1432608067700458825)
XLA Ops:
  0.6 38.2 %shard_map.77 = (bf16[64,1024]{1,0:T(8,128)(2,1)}, bf16[64,1024]{1,0:T(8,128)(2,1)}) custom-call(bf16[64,1024]{1,0:T(8,128)(2,1)} %bitcast.8, bf16[1024,1024]{1,0:T(8,128)(2,1)} %bitcast.6, bf16[1024,1024]{1,0:T(8,128)(2,1)} %bitcast.7, bf16[32,1024]{1,0:T(8,128)(2,1)} %bitcast.9, bf16[32,256]{1,0:T(8,128)(2,1)} %inverse_hbm.1, s32[2,16]{1,0:T(2,128)} %counts_hbm.1), custom_call_target="tpu_custom_call" | custom-call | tf_op jit(solution)/shard_map/pallas_call | solution.py:508
  38.8 1.7 %shard_map.78 = (bf16[64,1024]{1,0:T(8,128)(2,1)}, bf16[64,1024]{1,0:T(8,128)(2,1)}) custom-call(bf16[64,1024]{1,0:T(8,128)(2,1)} %get-tuple-element.6.mult_in, bf16[64,1024]{1,0:T(8,128)(2,1)} %get-tuple-element.7.resid_in), custom_call_target="tpu_custom_call" | custom-call | tf_op jit(solution)/shard_map/pallas_call | solution.py:547

commit v7 on v6

--- a/solution.py
+++ b/solution.py
@@ -204,17 +204,18 @@
             pl.semaphore_wait(barrier, total - 1)
         for f in pair:
             face_start(0, f)
-
-    get_modes.wait()
-    get_inverse.wait()
-    for f in range(FACES):
-        @pl.when(exists[f])
-        def _():
-            modes_copy(f, OPPOSITE[f]).start()
-    if direct:
-        to_column(inverse, sums)
-    else:
-        to_row(inverse, sums)
+        if pair == PAIRS[0]:
+            get_modes.wait()
+            get_inverse.wait()
+            for f in range(FACES):
+                @pl.when(exists[f])
+                def _(f=f):
+                    modes_copy(f, OPPOSITE[f]).start()
+            if direct:
+                to_column(inverse, sums)
+            else:
+                to_row(inverse, sums)
+
 
     get_counts.wait()
     counts = counts_ref[...].astype(F32).astype(BF16)

time: 40.7 us -> 40.5 us (level)
  no operation moved by 1% of the time
where the time goes in v7:
time: 40.5 us; the launch traced here: 40.3 us
  Pallas kernels  39.7 us (98%)
  between operations  0.64 us (2%)
    pallas_call x1, Pallas kernels, shards(): pl.pallas_call(functools.partial(kernel, rows, cols, direct), out_shape=[...  38 us
    pallas_call x1, Pallas kernels, shards(): pl.pallas_call(settle, out_shape=[jax.ShapeDtypeStruct((cases, width), BF...  1.68 us

profile of v7, /device:TPU:0, one launch (start us, length us, event | category | flops | bytes accessed | tf_op | source)
XLA Modules:
  0.0 40.3 jit_solution(12094374601554541451)
XLA Ops:
  0.6 38.0 %shard_map.77 = (bf16[64,1024]{1,0:T(8,128)(2,1)}, bf16[64,1024]{1,0:T(8,128)(2,1)}) custom-call(bf16[64,1024]{1,0:T(8,128)(2,1)} %bitcast.8, bf16[1024,1024]{1,0:T(8,128)(2,1)} %bitcast.6, bf16[1024,1024]{1,0:T(8,128)(2,1)} %bitcast.7, bf16[32,1024]{1,0:T(8,128)(2,1)} %bitcast.9, bf16[32,256]{1,0:T(8,128)(2,1)} %inverse_hbm.1, s32[2,16]{1,0:T(2,128)} %counts_hbm.1), custom_call_target="tpu_custom_call" | custom-call | tf_op jit(solution)/shard_map/pallas_call | solution.py:509
  38.7 1.7 %shard_map.78 = (bf16[64,1024]{1,0:T(8,128)(2,1)}, bf16[64,1024]{1,0:T(8,128)(2,1)}) custom-call(bf16[64,1024]{1,0:T(8,128)(2,1)} %get-tuple-element.6.mult_in, bf16[64,1024]{1,0:T(8,128)(2,1)} %get-tuple-element.7.resid_in), custom_call_target="tpu_custom_call" | custom-call | tf_op jit(solution)/shard_map/pallas_call | solution.py:548
